TPU v7x, 512 devices: a whole 4x8x8 slice. The times are simulated.
512 devices in a mesh: section: 4 (over z_hi), dp: 32 (over x, y), tensor: 4 (over z_lo, core).
Axes of the slice: x: 4, y: 8, z: 8 (z_hi: 4, z_lo: 2; z = z_hi * 2 + z_lo), core: 2. Of those that a mesh axis runs over, the one named last changes fastest.
Arguments:
- top_grad: bfloat16 [4, 2048, 8192], P(None, 'dp', 'tensor'), may hold values from -6 to 6
- stash: bfloat16 [4, 4, 2048, 8192], P('section', None, 'dp', 'tensor'), may hold values from -6 to 6
- value_grad: bfloat16 [4, 4, 2048, 512], P('section', None, 'dp', 'tensor'), may hold values from -6 to 6
- value_weight: bfloat16 [4, 512, 8192], P('section', 'dp', 'tensor'), may hold values from -0.25 to 0.25
- left_stats: float32 [4, 16, 512, 512], P('section', 'tensor', 'dp'), as said below
- right_stats: float32 [4, 16, 512, 512], P('section', 'tensor', 'dp'), as said below
- refresh: int32 [4, 4, 2], P('section', 'tensor'), may hold values from 0 to 3, as said below
- order: int32 [4], replicated, may hold values from 0 to 3, each once
Outputs:
- input_grad: bfloat16 [4, 4, 2048, 8192], P('section', None, 'dp', 'tensor')
- weight_grad: float32 [4, 512, 8192], P('section', 'dp', 'tensor')
- new_left: float32 [4, 16, 512, 512], P('section', 'tensor', 'dp')
- new_right: float32 [4, 16, 512, 512], P('section', 'tensor', 'dp')
- roots: float32 [4, 4, 4, 512, 512], P('section', 'tensor', None, 'dp')
Inputs may be any that keep to these rules, and one draw needn't show every extreme that they name: `refresh`: each row holds 2 consecutive block numbers modulo 4, from a start drawn for each row. `order`: A permutation of the micro-batches. `left_stats`: each matrix is symmetric positive definite. `right_stats`: each matrix is symmetric positive definite.
All inputs are finite; a program needn't handle non-finite values.
Results may differ from a plain program's by a relative error of at most 0.015.
Values may be sent and summed in bfloat16 or wider, within the bound.
No kernel may reach another device: no remote copies, remote signals or barrier semaphores. Data moves between devices by JAX's collectives and lax.ppermute only.
A program may use at most 64 MiB of HBM per device.

v0:
```python
import jax
import jax.numpy as jnp
from jax import lax
from jax.sharding import PartitionSpec as P

ITERS = 2


EPS = 1e-06


def from_behind(block, axis, distance):
    devices = range(lax.axis_size(axis))
    route = [(i - distance, i) for i in devices if i - distance in devices]
    return lax.ppermute(block, axis, route)


def inverse_root(statistic):
    order_size = statistic.shape[-1]
    scale = (
        jnp.sqrt(jnp.mean(statistic * statistic, axis=(-2, -1), keepdims=True) + EPS) * order_size
    )
    normed = statistic / scale
    identity = jnp.eye(order_size, dtype=statistic.dtype)
    result = jnp.broadcast_to(identity, statistic.shape)
    for step in range(ITERS):
        factor = (5.0 * identity - normed) * 0.25
        result = jnp.matmul(result, factor, precision=lax.Precision.HIGHEST)
        if step + 1 < ITERS:
            square = jnp.matmul(factor, factor, precision=lax.Precision.HIGHEST)
            fourth = jnp.matmul(square, square, precision=lax.Precision.HIGHEST)
            normed = jnp.matmul(fourth, normed, precision=lax.Precision.HIGHEST)
    return result


def per_device(top_grad, stash, value_grad, value_weight, left_stats, right_stats, refresh, order):
    micro, tok_dev, width_dev = top_grad.shape
    rows_own = value_weight.shape[1]
    block_count = left_stats.shape[1]
    kv_full = left_stats.shape[3]
    rows_total = micro * tok_dev
    n_data = lax.axis_size("dp")
    data_index = lax.axis_index("dp")
    n_section = lax.axis_size("section")
    section_index = lax.axis_index("section")
    value_full = lax.all_gather(value_grad[0], "tensor", axis=2, tiled=True)
    grads_flat = value_full.reshape(rows_total, kv_full)
    contribution = jnp.dot(
        grads_flat,
        lax.all_gather(value_weight[0], "dp", axis=0, tiled=True),
        preferred_element_type=jnp.float32,
    )
    contribution = contribution.reshape(micro, tok_dev, width_dev)
    carried = top_grad
    section_grad = top_grad
    for step in range(n_section):
        current = n_section - 1 - step
        updated = (carried.astype(jnp.float32) + contribution).astype(jnp.bfloat16)
        section_grad = jnp.where(section_index == current, updated, section_grad)
        if step + 1 < n_section:
            carried = from_behind(updated, "section", -1)
    paired = jnp.take(value_full, order, axis=0).reshape(rows_total, kv_full)
    inputs_flat = stash[0].reshape(rows_total, width_dev)
    partial_value = lax.dot_general(
        paired, inputs_flat, (((0,), (0,)), ((), ())), preferred_element_type=jnp.float32
    )
    own_grad = lax.psum_scatter(
        partial_value.astype(jnp.bfloat16), "dp", scatter_dimension=0, tiled=True
    ).astype(jnp.float32)
    own_rounded = own_grad.astype(jnp.bfloat16)
    own_blocks = own_rounded.reshape(rows_own, block_count, kv_full)
    shard_rows = lax.all_gather(own_rounded, "dp", axis=0, tiled=True)
    blocks = shard_rows.reshape(shard_rows.shape[0], block_count, kv_full)
    picked = lax.dynamic_slice_in_dim(blocks, data_index * rows_own, rows_own, 2)
    right_part = jnp.einsum("nbc,nbk->bck", picked, blocks, preferred_element_type=jnp.float32)
    cross = jnp.einsum("rbk,nbk->brn", own_blocks, blocks, preferred_element_type=jnp.float32)
    new_left = left_stats[0] + cross
    new_right = right_stats[0] + right_part
    both_sides = jnp.stack([new_left, new_right], axis=1)
    block_ids = refresh[0, 0]
    item_count = 2 * block_ids.shape[0]
    padding = jnp.zeros((n_data - block_count, 2, rows_own, kv_full), jnp.float32)
    outgoing = jnp.concatenate([both_sides, padding], axis=0)
    arrived = lax.all_to_all(
        outgoing.astype(jnp.bfloat16), "dp", split_axis=0, concat_axis=2, tiled=True
    ).astype(outgoing.dtype)
    wanted = jnp.any(block_ids == data_index)
    solved = lax.cond(wanted, inverse_root, jnp.zeros_like, arrived[0])
    returned = lax.all_to_all(
        solved[None].astype(jnp.bfloat16), "dp", split_axis=2, concat_axis=0, tiled=True
    ).astype(jnp.float32)
    roots = jnp.take(returned, block_ids, axis=0).reshape(item_count, rows_own, kv_full)
    return (section_grad[None], own_grad[None], new_left[None], new_right[None], roots[None, None])


def solution(mesh):
    return jax.shard_map(
        per_device,
        mesh=mesh,
        in_specs=(
            P(None, "dp", "tensor"),
            P("section", None, "dp", "tensor"),
            P("section", None, "dp", "tensor"),
            P("section", "dp", "tensor"),
            P("section", "tensor", "dp", None),
            P("section", "tensor", "dp", None),
            P("section", "tensor", None),
            P(),
        ),
        out_specs=(
            P("section", None, "dp", "tensor"),
            P("section", "dp", "tensor"),
            P("section", "tensor", "dp", None),
            P("section", "tensor", "dp", None),
            P("section", "tensor", None, "dp", None),
        ),
        check_vma=False,
    )
```

profile of v0, /device:TPU:8, one launch (start us, length us, event | category | flops | bytes accessed | tf_op | source)
XLA Modules:
  0.0 545.9 jit_solution(288234667140724442)
XLA Ops:
  7.2 0.0 reduce-scatter.2.cloned.1.call-start
  7.2 0.7 compare_select_fusion.2
  8.0 0.7 compare_and_fusion.1
  8.6 6.8 %all-gather = bf16[1,4,64,512]{3,2,1,0:T(8,128)(2,1)S(1)} all-gather(bf16[1,4,64,128]{3,2,1,0:T(8,128)(2,1)} %param.12), channel_id=2, replica_groups=mesh['section'=4,'dp'=32,'tensor'=4] {'tensor'}, dimensions={3}, use_global_device_ids=true | all-gather | bytes 327680 | tf_op jit(solution)/shard_map/all_gather | solution.py:46
  15.5 0.6 gather_fusion
  16.0 0.1 broadcast_select_fusion
  16.1 2.1 convolution_convert_fusion
  18.2 0.0 reduce-scatter.2.cloned.1.call-update
  18.3 0.0 all-gather.7.cloned.1.call-start
  18.3 0.7 all-gather.7.cloned.1.call-update
  19.0 0.0 all-gather.5.cloned.1.call-start
  19.1 223.9 %reduce-scatter.2.cloned.1.call-done = bf16[16,2048]{1,0:T(8,128)(2,1)} async-done(((bf16[512,2048]{1,0:T(8,128)(2,1)}), bf16[16,2048]{1,0:T(8,128)(2,1)}) %reduce-scatter.2.cloned.1.call-update) | async-done | bytes 65552 | tf_op jit(solution)/shard_map/reduce_scatter | solution.py:67
  242.9 85.4 %all-gather.7.cloned.1.call-done = bf16[1,512,2048]{2,1,0:T(8,128)(2,1)} async-done(((bf16[1,16,2048]{2,1,0:T(8,128)(2,1)}), bf16[1,512,2048]{2,1,0:T(8,128)(2,1)}) %all-gather.7.cloned.1.call-update) | async-done | bytes 2097168 | tf_op jit(solution)/shard_map/all_gather | solution.py:50
  328.3 3.5 add_convert_fusion.3
  331.9 1.4 collective-permute-start
  333.3 79.4 %all-gather.5.cloned.1.call-done = bf16[512,2048]{1,0:T(8,128)(2,1)} async-done(((bf16[16,2048]{1,0:T(8,128)(2,1)}), bf16[512,2048]{1,0:T(8,128)(2,1)}) %all-gather.5.cloned.1.call-update) | async-done | bytes 2097168 | tf_op jit(solution)/shard_map/all_gather | solution.py:72
  412.7 4.5 reshape.134
  417.2 1.5 constant_dynamic-slice_fusion
  418.8 2.0 fusion.26
  420.8 0.7 fusion.29
  421.6 1.1 concatenate.3.clone
  422.7 7.2 %all-to-all-start = ((bf16[32,2,16,512]{3,2,1,0:T(8,128)(2,1)}), bf16[32,2,16,512]{3,2,1,0:T(8,128)(2,1)}, u32[]{:S(2)}, u32[]{:S(2)}) async-start(bf16[32,2,16,512]{3,2,1,0:T(8,128)(2,1)} %concatenate.3.clone), calls=%async_computation.1 | async-start | bytes 2097152 | tf_op jit(solution)/shard_map/all_to_all | solution.py:84
  429.9 2.5 add_convert_fusion.2
  432.4 1.3 collective-permute-start.1
  433.7 0.6 compare_and_fusion
  435.0 19.3 %all-to-all-done = bf16[32,2,16,512]{3,2,1,0:T(8,128)(2,1)} async-done(((bf16[32,2,16,512]{3,2,1,0:T(8,128)(2,1)}), bf16[32,2,16,512]{3,2,1,0:T(8,128)(2,1)}, u32[]{:S(2)}, u32[]{:S(2)}) %all-to-all-start) | async-done | bytes 1048608 | tf_op jit(solution)/shard_map/all_to_all | solution.py:84
  454.3 23.5 %conditional.1 = (bf16[2,512,512]{2,1,0:T(8,128)(2,1)}) conditional(s32[]{:T(128)} %convert_element_type.76, () %tuple.14, bf16[1,2,32,16,512]{4,3,1,2,0:T(8,128)(2,1)} %bitcast.16), branch_computations={%region_2.3_spmd, %region_3.5_spmd} | conditional | flops 16113991680 | bytes 34603064 | solution.py:88
  454.3 1.5 copy_convert_fusion
  455.8 0.1 fusion.12
  455.9 1.6 multiply_reduce_fusion
  457.5 4.0 fusion.3
  461.6 3.5 fusion.39
  465.1 3.7 fusion.17
  468.8 0.1 fusion.13
  468.9 4.1 fusion.4
  473.1 4.7 fusion
  477.7 3.3 copy.52
  481.0 4.5 all-to-all-start.1
  485.6 2.5 add_convert_fusion.1
  488.0 1.3 collective-permute-start.2
  489.3 0.1 broadcast_in_dim.57
  489.4 0.1 broadcast_in_dim.58
  489.5 0.7 bitcast_convert_fusion
  490.2 42.8 %collective-permute-done.2 = bf16[4,64,2048]{2,1,0:T(8,128)(2,1)} collective-permute-done((bf16[4,64,2048]{2,1,0:T(8,128)(2,1)}, bf16[4,64,2048]{2,1,0:T(8,128)(2,1)}, u32[]{:S(2)}, u32[]{:S(2)}) %collective-permute-start.2) | collective-permute-done | bytes 1048608 | tf_op jit(solution)/shard_map/ppermute | solution.py:15
  532.9 2.8 fusion.33
  535.8 2.1 convert_bitcast_fusion
  537.9 0.7 gather_fusion.1
  538.6 0.7 broadcast_select_fusion.1
  (28 shorter events, 0.2 us)
Async XLA Ops:
  7.2 9.0 %copy-start = (bf16[1,4,64,2048]{3,2,1,0:T(8,128)(2,1)S(1)}, bf16[1,4,64,2048]{3,2,1,0:T(8,128)(2,1)}, u32[]{:S(2)}) copy-start(bf16[1,4,64,2048]{3,2,1,0:T(8,128)(2,1)} %param.11) | copy-start | bytes 3145732
  7.2 235.7 %reduce-scatter.2.cloned.1.call-start = ((), (), s32[]{:S(2)}) async-start(), calls=%async_computation.3 | async-start | bytes 2162688 | tf_op jit(solution)/shard_map/reduce_scatter | solution.py:67
  18.3 310.1 %all-gather.7.cloned.1.call-start = ((), (), s32[]{:S(2)}) async-start(), calls=%async_computation.5 | async-start | bytes 2162688 | tf_op jit(solution)/shard_map/all_gather | solution.py:50
  19.0 393.7 %all-gather.5.cloned.1.call-start = ((), (), s32[]{:S(2)}) async-start(), calls=%async_computation.4 | async-start | bytes 2162688 | tf_op jit(solution)/shard_map/all_gather | solution.py:72
  331.9 86.9 %copy-start.5 = (f32[1,4,16,512]{3,2,1,0:T(8,128)S(1)}, f32[1,4,16,512]{3,2,1,0:T(8,128)}, u32[]{:S(2)}) copy-start(f32[1,4,16,512]{3,2,1,0:T(8,128)} %param.15) | copy-start | bytes 393220
  331.9 98.0 %collective-permute-start = (bf16[4,64,2048]{2,1,0:T(8,128)(2,1)}, bf16[4,64,2048]{2,1,0:T(8,128)(2,1)}, u32[]{:S(2)}, u32[]{:S(2)}) collective-permute-start(bf16[4,64,2048]{2,1,0:T(8,128)(2,1)} %get-tuple-element.13), channel_id=1, source_target_pairs={{128,0},{256,128},{384,256},{129,1},{257,129},{385,257},{130,2},{2... | collective-permute-start | bytes 3145736 | tf_op jit(solution)/shard_map/ppermute | solution.py:15
  417.2 3.6 copy-start.1
  417.2 3.6 copy-start.2
  417.2 3.6 copy-start.6
  420.8 1.9 copy-start.3
  421.5 1.2 copy-start.4
  422.7 31.6 %all-to-all-start = ((bf16[32,2,16,512]{3,2,1,0:T(8,128)(2,1)}), bf16[32,2,16,512]{3,2,1,0:T(8,128)(2,1)}, u32[]{:S(2)}, u32[]{:S(2)}) async-start(bf16[32,2,16,512]{3,2,1,0:T(8,128)(2,1)} %concatenate.3.clone), calls=%async_computation.1 | async-start | bytes 2097152 | tf_op jit(solution)/shard_map/all_to_all | solution.py:84
  429.9 3.8 copy-start.7
  432.4 53.1 %collective-permute-start.1 = (bf16[4,64,2048]{2,1,0:T(8,128)(2,1)}, bf16[4,64,2048]{2,1,0:T(8,128)(2,1)}, u32[]{:S(2)}, u32[]{:S(2)}) collective-permute-start(bf16[4,64,2048]{2,1,0:T(8,128)(2,1)} %add_convert_fusion.2), channel_id=1, source_target_pairs={{128,0},{256,128},{384,256},{129,1},{257,129},{385,257},{130,2},{2... | collective-permute-start | bytes 3145736 | tf_op jit(solution)/shard_map/ppermute | solution.py:15
  481.0 54.8 %all-to-all-start.1 = ((bf16[1,2,512,512]{3,1,0,2:T(2,128)(2,1)}), bf16[1,2,512,512]{3,1,0,2:T(2,128)(2,1)}, u32[]{:S(2)}, u32[]{:S(2)}) async-start(bf16[1,2,512,512]{3,1,0,2:T(2,128)(2,1)} %bitcast.72), calls=%async_computation.2 | async-start | bytes 2097152 | tf_op jit(solution)/shard_map/all_to_all | solution.py:89
  488.0 44.9 %collective-permute-start.2 = (bf16[4,64,2048]{2,1,0:T(8,128)(2,1)}, bf16[4,64,2048]{2,1,0:T(8,128)(2,1)}, u32[]{:S(2)}, u32[]{:S(2)}) collective-permute-start(bf16[4,64,2048]{2,1,0:T(8,128)(2,1)} %add_convert_fusion.1), channel_id=1, source_target_pairs={{128,0},{256,128},{384,256},{129,1},{257,129},{385,257},{130,2},{2... | collective-permute-start | bytes 3145736 | tf_op jit(solution)/shard_map/ppermute | solution.py:15
Sparse Core Ops, SparseCore 0:
  18.4 224.4 reduce-scatter.1
  246.6 81.7 all-gather.6
  332.0 80.6 all-gather.4
where the time goes:
time: 547 us; the launch traced here: 546 us
  waiting for transfers between devices  451 us (82%)
  matrix products  28.4 us (5%)
  other arithmetic  16.9 us (3%)
  starting transfers between devices  15.8 us (3%)
  between operations  14.6 us (3%)
  local copies, waits for them, and re-layouts  11.9 us (2%)
  blocking collectives  6.84 us (1%)
    reduce_scatter x1, waiting for transfers between devices, per_device(): lax.psum_scatter(partial_value.astype(jnp.bfloat16), 'dp', scatter_dimens...  224 us
    all_gather x1, waiting for transfers between devices, per_device(): lax.all_gather(value_weight[0], 'dp', axis=0, tiled=True)  85.4 us
    all_gather x1, waiting for transfers between devices, per_device(): shard_rows = lax.all_gather(own_rounded, 'dp', axis=0, tiled=True)  79.4 us
    ppermute x3, waiting for transfers between devices, from_behind(): return lax.ppermute(block, axis, route)  42.8 us
    all_to_all x1, waiting for transfers between devices, per_device(): lax.all_to_all(outgoing.astype(jnp.bfloat16), 'dp', split_axis=0, concat_...  19.3 us
  transfers between devices with their start and end apart: 8, of which 5 were waited for; matrix products, arithmetic and copies ran while one was open for 9% of the time, Pallas kernels for 0%

commit v1 on v0

v1 whole, which is shorter than its diff:
```python
import jax
import jax.numpy as jnp
from jax import lax
from jax.sharding import PartitionSpec as P

EPS = 1e-06

NX = 4
NY = 8
X_GROUPS = [[x * NY + y for x in range(NX)] for y in range(NY)]
Y_GROUPS = [[x * NY + y for y in range(NY)] for x in range(NX)]
CHUNKS = 4


def exchange(block, groups):
    return lax.all_to_all(block, "dp", 0, 0, axis_index_groups=groups, tiled=True)


def spread(block, count, groups):
    return exchange(jnp.broadcast_to(block[None], (count, *block.shape)), groups)


def root_rows(stat, row_of):
    size = stat.shape[-1]
    scale = jnp.sqrt(jnp.mean(stat * stat, axis=(-2, -1), keepdims=True) + EPS) * size
    normed = stat / scale
    mine = row_of(normed)
    identity = row_of(jnp.broadcast_to(jnp.eye(size, dtype=jnp.float32), stat.shape))
    matrix = normed.astype(jnp.bfloat16)
    term = mine
    for _ in range(5):
        term = 1.25 * term - 0.25 * jnp.einsum(
            "srk,skc->src",
            term.astype(jnp.bfloat16),
            matrix,
            preferred_element_type=jnp.float32,
        )
    return 0.25 * (6.25 * identity - 1.25 * mine - term)


def per_device(top_grad, stash, value_grad, value_weight, left_stats, right_stats, refresh, order):
    micro, tok_dev, width = top_grad.shape
    rows_own = value_weight.shape[1]
    blocks = left_stats.shape[1]
    kv = left_stats.shape[3]
    tokens = micro * tok_dev
    n_section = lax.axis_size("section")
    section = lax.axis_index("section")
    y_index = lax.axis_index("dp") % NY

    value_full = lax.all_gather(value_grad[0], "tensor", axis=2, tiled=True)

    weight_x = spread(value_weight[0], NX, X_GROUPS)
    weight = lax.all_gather(weight_x, "dp", axis=0, axis_index_groups=Y_GROUPS)
    weight = weight.transpose(1, 0, 2, 3).reshape(kv, width)

    paired = jnp.take(value_full, order, axis=0).reshape(tokens, kv)
    inputs = stash[0].reshape(tokens, width)
    partial = jnp.stack(
        [
            lax.dot_general(
                paired,
                inputs[:, b * kv : (b + 1) * kv],
                (((0,), (0,)), ((), ())),
                preferred_element_type=jnp.float32,
            ).astype(jnp.bfloat16)
            for b in range(blocks)
        ]
    )
    over_x = jnp.sum(exchange(partial, X_GROUPS).astype(jnp.float32), axis=0).astype(jnp.bfloat16)
    by_y = over_x.reshape(NX, NY, rows_own, kv).transpose(1, 0, 2, 3)
    own = jnp.sum(exchange(by_y, Y_GROUPS).astype(jnp.float32), axis=0)
    own_rounded = own.astype(jnp.bfloat16)
    block = spread(own_rounded, NY, Y_GROUPS).transpose(1, 0, 2, 3).reshape(kv, kv)

    stats = jnp.stack([left_stats[0], right_stats[0]], axis=1).astype(jnp.bfloat16)
    stats = exchange(stats, X_GROUPS)
    stats = lax.all_gather(stats, "dp", axis=0, axis_index_groups=Y_GROUPS)
    stats = stats.transpose(2, 1, 0, 3, 4).reshape(2, kv, kv).astype(jnp.float32)

    def row_of(arr):
        view = arr.reshape(2, NX, NY, rows_own, kv)
        picked = lax.dynamic_index_in_dim(view, y_index, 2, keepdims=False)
        return picked.reshape(2, NX * rows_own, kv)

    left_gram = lax.dot_general(
        block, block, (((1,), (1,)), ((), ())), preferred_element_type=jnp.float32
    )
    right_gram = lax.dot_general(
        block, block, (((0,), (0,)), ((), ())), preferred_element_type=jnp.float32
    )
    grams = jnp.stack([left_gram, right_gram])
    roots_mine = root_rows(stats + grams, row_of)
    grams_mine = row_of(grams)
    sent = jnp.concatenate(
        [own_rounded.reshape(1, NX, rows_own, kv)]
        + [a.astype(jnp.bfloat16).reshape(2, NX, rows_own, kv) for a in (grams_mine, roots_mine)],
        axis=0,
    ).transpose(1, 0, 2, 3)
    back = exchange(sent, X_GROUPS).astype(jnp.float32)
    weight_grad = back[:, 0].transpose(1, 0, 2).reshape(rows_own, width)
    new_left = left_stats[0] + back[:, 1]
    new_right = right_stats[0] + back[:, 2]
    roots = jnp.take(back[:, 3:5], refresh[0, 0], axis=0).reshape(-1, rows_own, kv)

    grads_flat = value_full.reshape(tokens, kv)
    top = top_grad.reshape(tokens, width)
    cols = width // CHUNKS
    pieces = []
    for k in range(CHUNKS):
        part = slice(k * cols, (k + 1) * cols)
        contribution = jnp.dot(
            grads_flat, weight[:, part], preferred_element_type=jnp.float32
        )
        held = (top[:, part].astype(jnp.float32) + contribution).astype(jnp.bfloat16)
        for below in range(n_section - 2, -1, -1):
            arrived = lax.ppermute(held, "section", [(below + 1, below)])
            updated = (arrived.astype(jnp.float32) + contribution).astype(jnp.bfloat16)
            held = jnp.where(section == below, updated, held)
        pieces.append(held)
    section_grad = jnp.concatenate(pieces, axis=1).reshape(micro, tok_dev, width)
    return (
        section_grad[None],
        weight_grad[None],
        new_left[None],
        new_right[None],
        roots[None, None],
    )


def solution(mesh):
    return jax.shard_map(
        per_device,
        mesh=mesh,
        in_specs=(
            P(None, "dp", "tensor"),
            P("section", None, "dp", "tensor"),
            P("section", None, "dp", "tensor"),
            P("section", "dp", "tensor"),
            P("section", "tensor", "dp", None),
            P("section", "tensor", "dp", None),
            P("section", "tensor", None),
            P(),
        ),
        out_specs=(
            P("section", None, "dp", "tensor"),
            P("section", "dp", "tensor"),
            P("section", "tensor", "dp", None),
            P("section", "tensor", "dp", None),
            P("section", "tensor", None, "dp", None),
        ),
        check_vma=False,
    )
```

time: 547 us -> 262 us (0.48)
  the two profiles are of different devices: /device:TPU:8 before, /device:TPU:1 now
where the time goes in v1:
time: 262 us; the launch traced here: 261 us
  waiting for transfers between devices  157 us (60%)
  starting transfers between devices  36.1 us (14%)
  other arithmetic  22.6 us (9%)
  between operations  14.7 us (6%)
  local copies, waits for them, and re-layouts  13.6 us (5%)
  blocking collectives  11.2 us (4%)
  matrix products  5.76 us (2%)
    ppermute x12, waiting for transfers between devices, per_device(): arrived = lax.ppermute(held, 'section', [(below + 1, below)])  82.7 us
    all_to_all x6, waiting for transfers between devices, exchange(): lax.all_to_all(block, 'dp', 0, 0, axis_index_groups=groups, tiled=True)  60.9 us
    all_to_all x6, starting transfers between devices, exchange(): lax.all_to_all(block, 'dp', 0, 0, axis_index_groups=groups, tiled=True)  23.3 us
    ppermute x12, starting transfers between devices, per_device(): arrived = lax.ppermute(held, 'section', [(below + 1, below)])  12.8 us
    all_gather x1, waiting for transfers between devices, per_device(): weight = lax.all_gather(weight_x, 'dp', axis=0, axis_index_groups=Y_GROUPS)  12 us
    all_gather x1, blocking collectives, per_device(): value_full = lax.all_gather(value_grad[0], 'tensor', axis=2, tiled=True)  11.2 us
    select_n x6, other arithmetic, per_device(): held = jnp.where(section == below, updated, held)  7.88 us
  transfers between devices with their start and end apart: 20, of which 10 were waited for; matrix products, arithmetic and copies ran while one was open for 10% of the time, Pallas kernels for 0%

profile of v1, /device:TPU:1, one launch (start us, length us, event | category | flops | bytes accessed | tf_op | source)
XLA Modules:
  0.0 261.0 jit_solution(5743001892382420491)
XLA Ops:
  7.2 1.1 convert_bitcast_fusion.1
  8.9 4.8 %all-to-all-start.4 = ((bf16[4,2,16,512]{3,2,1,0:T(8,128)(2,1)}), bf16[4,2,16,512]{3,2,1,0:T(8,128)(2,1)S(1)}, u32[]{:S(2)}, u32[]{:S(2)}) async-start(bf16[4,2,16,512]{3,2,1,0:T(8,128)(2,1)} %pad_maximum_fusion.3), calls=%async_computation.4 | async-start | bytes 262144 | tf_op jit(solution)/shard_map/all_to_all | solution.py:16
  15.1 11.2 %all-gather = bf16[1,4,64,512]{3,2,1,0:T(8,128)(2,1)S(1)} all-gather(bf16[1,4,64,128]{3,2,1,0:T(8,128)(2,1)} %param.10), channel_id=2, replica_groups=mesh['section'=4,'dp'=32,'tensor'=4] {'tensor'}, dimensions={3}, use_global_device_ids=true | all-gather | bytes 327680 | tf_op jit(solution)/shard_map/all_gather | solution.py:51
  28.5 1.6 pad_maximum_fusion
  30.8 4.5 %all-to-all-start.1 = ((bf16[4,512,512]{2,1,0:T(8,128)(2,1)}), bf16[4,512,512]{2,1,0:T(8,128)(2,1)S(1)}, u32[]{:S(2)}, u32[]{:S(2)}) async-start(bf16[4,512,512]{2,1,0:T(8,128)(2,1)} %pad_maximum_fusion), calls=%async_computation.1 | async-start | bytes 4194304 | tf_op jit(solution)/shard_map/all_to_all | solution.py:16
  35.2 0.7 all-gather.8.cloned.1.call-update
  36.0 25.3 %all-to-all-done.1 = bf16[4,512,512]{2,1,0:T(8,128)(2,1)S(1)} async-done(((bf16[4,512,512]{2,1,0:T(8,128)(2,1)}), bf16[4,512,512]{2,1,0:T(8,128)(2,1)S(1)}, u32[]{:S(2)}, u32[]{:S(2)}) %all-to-all-start.1) | async-done | bytes 2097184 | tf_op jit(solution)/shard_map/all_to_all | solution.py:16
  61.2 0.7 broadcast_in_dim.50
  62.0 3.4 %all-to-all-start = ((bf16[4,16,2048]{2,1,0:T(8,128)(2,1)}), bf16[4,16,2048]{2,1,0:T(8,128)(2,1)S(1)}, u32[]{:S(2)}, u32[]{:S(2)}) async-start(bf16[4,16,2048]{2,1,0:T(8,128)(2,1)} %broadcast_in_dim.50), calls=%async_computation | async-start | bytes 524288 | tf_op jit(solution)/shard_map/all_to_all | solution.py:16
  66.0 0.8 copy.41
  66.9 4.0 %all-to-all-done = bf16[4,16,2048]{2,1,0:T(8,128)(2,1)S(1)} async-done(((bf16[4,16,2048]{2,1,0:T(8,128)(2,1)}), bf16[4,16,2048]{2,1,0:T(8,128)(2,1)S(1)}, u32[]{:S(2)}, u32[]{:S(2)}) %all-to-all-start) | async-done | bytes 262176 | tf_op jit(solution)/shard_map/all_to_all | solution.py:16
  70.9 3.5 %all-to-all-start.2 = ((bf16[8,4,16,512]{3,2,1,0:T(8,128)(2,1)}), bf16[8,4,16,512]{3,2,1,0:T(8,128)(2,1)S(1)}, u32[]{:S(2)}, u32[]{:S(2)}) async-start(bf16[8,4,16,512]{3,2,1,0:T(8,128)(2,1)} %copy.41), calls=%async_computation.2 | async-start | bytes 1048576 | tf_op jit(solution)/shard_map/all_to_all | solution.py:16
  75.2 15.2 %all-to-all-done.2 = bf16[8,4,16,512]{3,2,1,0:T(8,128)(2,1)S(1)} async-done(((bf16[8,4,16,512]{3,2,1,0:T(8,128)(2,1)}), bf16[8,4,16,512]{3,2,1,0:T(8,128)(2,1)S(1)}, u32[]{:S(2)}, u32[]{:S(2)}) %all-to-all-start.2) | async-done | bytes 524320 | tf_op jit(solution)/shard_map/all_to_all | solution.py:16
  90.5 0.9 broadcast_in_dim.56
  91.3 3.5 %all-to-all-start.3 = ((bf16[8,4,16,512]{3,2,1,0:T(8,128)(2,1)}), bf16[8,4,16,512]{3,2,1,0:T(8,128)(2,1)S(1)}, u32[]{:S(2)}, u32[]{:S(2)}) async-start(bf16[8,4,16,512]{3,2,1,0:T(8,128)(2,1)} %broadcast_in_dim.56), calls=%async_computation.3 | async-start | bytes 1048576 | tf_op jit(solution)/shard_map/all_to_all | solution.py:16
  94.9 0.7 convert_multiply_fusion
  95.6 1.5 convert_bitcast_fusion
  97.1 1.6 copy.47
  98.8 16.0 %all-to-all-done.3 = bf16[8,4,16,512]{3,2,1,0:T(8,128)(2,1)S(1)} async-done(((bf16[8,4,16,512]{3,2,1,0:T(8,128)(2,1)}), bf16[8,4,16,512]{3,2,1,0:T(8,128)(2,1)S(1)}, u32[]{:S(2)}, u32[]{:S(2)}) %all-to-all-start.3) | async-done | bytes 524320 | tf_op jit(solution)/shard_map/all_to_all | solution.py:16
  115.8 0.7 copy-done.7
  117.4 0.7 copy-done.6
  119.0 1.0 fusion.11
  120.0 12.0 %all-gather.6.cloned.1.call-done = bf16[32,16,2048]{2,1,0:T(8,128)(2,1)} async-done(((bf16[4,16,2048]{2,1,0:T(8,128)(2,1)}), bf16[32,16,2048]{2,1,0:T(8,128)(2,1)}) %all-gather.6.cloned.1.call-update) | async-done | bytes 2097168 | tf_op jit(solution)/shard_map/all_gather | solution.py:54
  132.0 1.7 copy.40
  139.8 1.3 collective-permute-start.2
  141.5 58.3 %collective-permute-done.2 = bf16[256,512]{1,0:T(8,128)(2,1)S(1)} collective-permute-done((bf16[256,512]{1,0:T(8,128)(2,1)S(1)}, bf16[256,512]{1,0:T(8,128)(2,1)S(1)}, u32[]{:S(2)}, u32[]{:S(2)}) %collective-permute-start.2) | collective-permute-done | bytes 262176 | tf_op jit(solution)/shard_map/ppermute | solution.py:117
  199.8 1.5 fusion.27
  201.3 1.5 collective-permute-start.4
  202.9 0.7 maximum_bitcast_fusion
  203.6 3.6 %all-to-all-start.5 = ((bf16[4,5,16,512]{3,2,1,0:T(8,128)(2,1)}), bf16[4,5,16,512]{3,2,1,0:T(8,128)(2,1)S(1)}, u32[]{:S(2)}, u32[]{:S(2)}) async-start(bf16[4,5,16,512]{3,2,1,0:T(8,128)(2,1)} %maximum_bitcast_fusion), calls=%async_computation.5 | async-start | bytes 655360 | tf_op jit(solution)/shard_map/all_to_all | solution.py:16
  207.2 1.4 collective-permute-start.10
  208.6 1.3 collective-permute-start.7
  209.9 2.0 fusion.29
  211.9 1.3 collective-permute-start.5
  213.8 0.7 slice.83
  214.5 2.2 gather_fusion.1
  216.7 1.8 broadcast_select_fusion
  218.5 9.1 %collective-permute-done.5 = bf16[256,512]{1,0:T(8,128)(2,1)} collective-permute-done((bf16[256,512]{1,0:T(8,128)(2,1)}, bf16[256,512]{1,0:T(8,128)(2,1)}, u32[]{:S(2)}, u32[]{:S(2)}) %collective-permute-start.5) | collective-permute-done | bytes 262176 | tf_op jit(solution)/shard_map/ppermute | solution.py:117
  227.6 2.6 fusion.30
  230.2 1.3 collective-permute-start.11
  231.5 1.3 collective-permute-start.8
  232.9 0.7 broadcast_in_dim_reshape.8
  233.7 1.8 fusion.42
  235.5 10.3 %collective-permute-done.11 = bf16[256,512]{1,0:T(8,128)(2,1)S(1)} collective-permute-done((bf16[256,512]{1,0:T(8,128)(2,1)}, bf16[256,512]{1,0:T(8,128)(2,1)S(1)}, u32[]{:S(2)}, u32[]{:S(2)}) %collective-permute-start.11) | collective-permute-done | bytes 262176 | tf_op jit(solution)/shard_map/ppermute | solution.py:117
  245.8 0.7 copy-done.21
  246.5 5.0 %collective-permute-done.8 = bf16[256,512]{1,0:T(8,128)(2,1)} collective-permute-done((bf16[256,512]{1,0:T(8,128)(2,1)}, bf16[256,512]{1,0:T(8,128)(2,1)}, u32[]{:S(2)}, u32[]{:S(2)}) %collective-permute-start.8) | collective-permute-done | bytes 262176 | tf_op jit(solution)/shard_map/ppermute | solution.py:117
  251.5 1.6 fusion.33
  253.1 1.1 pad_maximum_fusion.2
  (108 shorter events, 16.0 us)
Async XLA Ops:
  7.2 20.0 %copy-start.15 = (bf16[1,4,64,2048]{3,2,1,0:T(8,128)(2,1)S(1)}, bf16[1,4,64,2048]{3,2,1,0:T(8,128)(2,1)}, u32[]{:S(2)}) copy-start(bf16[1,4,64,2048]{3,2,1,0:T(8,128)(2,1)} %param.9) | copy-start | bytes 3145732
  8.9 21.2 %all-to-all-start.4 = ((bf16[4,2,16,512]{3,2,1,0:T(8,128)(2,1)}), bf16[4,2,16,512]{3,2,1,0:T(8,128)(2,1)S(1)}, u32[]{:S(2)}, u32[]{:S(2)}) async-start(bf16[4,2,16,512]{3,2,1,0:T(8,128)(2,1)} %pad_maximum_fusion.3), calls=%async_computation.4 | async-start | bytes 262144 | tf_op jit(solution)/shard_map/all_to_all | solution.py:16
  30.1 0.7 copy-start.20
  30.1 31.1 %copy-start.22 = (bf16[1,16,2048]{2,1,0:T(8,128)(2,1)S(1)}, bf16[1,16,2048]{2,1,0:T(8,128)(2,1)}, u32[]{:S(2)}) copy-start(bf16[1,16,2048]{2,1,0:T(8,128)(2,1)} %param.11) | copy-start | bytes 196612
  30.8 30.5 %all-to-all-start.1 = ((bf16[4,512,512]{2,1,0:T(8,128)(2,1)}), bf16[4,512,512]{2,1,0:T(8,128)(2,1)S(1)}, u32[]{:S(2)}, u32[]{:S(2)}) async-start(bf16[4,512,512]{2,1,0:T(8,128)(2,1)} %pad_maximum_fusion), calls=%async_computation.1 | async-start | bytes 4194304 | tf_op jit(solution)/shard_map/all_to_all | solution.py:16
  35.2 60.4 %all-gather.8.cloned.1.call-start = ((), (), s32[]{:S(2)}) async-start(), calls=%async_computation.7 | async-start | bytes 1179648 | tf_op jit(solution)/shard_map/all_gather | solution.py:78
  62.0 8.9 %all-to-all-start = ((bf16[4,16,2048]{2,1,0:T(8,128)(2,1)}), bf16[4,16,2048]{2,1,0:T(8,128)(2,1)S(1)}, u32[]{:S(2)}, u32[]{:S(2)}) async-start(bf16[4,16,2048]{2,1,0:T(8,128)(2,1)} %broadcast_in_dim.50), calls=%async_computation | async-start | bytes 524288 | tf_op jit(solution)/shard_map/all_to_all | solution.py:16
  65.4 9.8 %copy-start.23 = (s32[1,1,2]{2,1,0:T(1,128)S(1)}, s32[1,1,2]{2,1,0:T(1,128)}, u32[]{:S(2)}) copy-start(s32[1,1,2]{2,1,0:T(1,128)} %param.14) | copy-start | bytes 28
  70.9 3.6 %copy-start.14 = (bf16[4,16,2048]{2,1,0:T(8,128)(2,1)}, bf16[4,16,2048]{2,1,0:T(8,128)(2,1)S(1)}, u32[]{:S(2)}) copy-start(bf16[4,16,2048]{2,1,0:T(8,128)(2,1)S(1)} %all-to-all-done) | copy-start | bytes 786436
  70.9 19.5 %all-to-all-start.2 = ((bf16[8,4,16,512]{3,2,1,0:T(8,128)(2,1)}), bf16[8,4,16,512]{3,2,1,0:T(8,128)(2,1)S(1)}, u32[]{:S(2)}, u32[]{:S(2)}) async-start(bf16[8,4,16,512]{3,2,1,0:T(8,128)(2,1)} %copy.41), calls=%async_computation.2 | async-start | bytes 1048576 | tf_op jit(solution)/shard_map/all_to_all | solution.py:16
  74.4 57.7 %all-gather.6.cloned.1.call-start = ((), (), s32[]{:S(2)}) async-start(), calls=%async_computation.6 | async-start | bytes 2359296 | tf_op jit(solution)/shard_map/all_gather | solution.py:54
  91.3 23.5 %all-to-all-start.3 = ((bf16[8,4,16,512]{3,2,1,0:T(8,128)(2,1)}), bf16[8,4,16,512]{3,2,1,0:T(8,128)(2,1)S(1)}, u32[]{:S(2)}, u32[]{:S(2)}) async-start(bf16[8,4,16,512]{3,2,1,0:T(8,128)(2,1)} %broadcast_in_dim.56), calls=%async_computation.3 | async-start | bytes 1048576 | tf_op jit(solution)/shard_map/all_to_all | solution.py:16
  115.3 1.2 copy-start.7
  115.8 1.6 copy-start.4
  116.5 1.6 copy-start.6
  117.4 1.4 copy-start.11
  133.8 1.2 copy-start.2
  134.7 65.1 %copy-start = (f32[256,512]{1,0:T(8,128)}, f32[256,512]{1,0:T(8,128)S(1)}, u32[]{:S(2)}) copy-start(f32[256,512]{1,0:T(8,128)S(1)} %fusion.19) | copy-start | bytes 1572868
  135.0 1.1 copy-start.17
  135.4 1.0 collective-permute-start
  136.4 4.7 %copy-start.12 = (f32[2,4,1,16,512]{4,3,1,0,2:T(8,128)S(1)}, f32[2,4,1,16,512]{4,3,1,0,2:T(8,128)}, u32[]{:S(2)}) copy-start(f32[2,4,1,16,512]{4,3,1,0,2:T(8,128)} %copy-done.11) | copy-start | bytes 786436
  136.4 4.7 %copy-start.18 = (f32[4,1,16,512]{3,2,0,1:T(8,128)S(1)}, f32[4,1,16,512]{3,2,0,1:T(8,128)}, u32[]{:S(2)}) copy-start(f32[4,1,16,512]{3,2,0,1:T(8,128)} %convert_multiply_fusion) | copy-start | bytes 393220
  136.6 3.0 %collective-permute-start.1 = (bf16[256,512]{1,0:T(8,128)(2,1)S(1)}, bf16[256,512]{1,0:T(8,128)(2,1)S(1)}, u32[]{:S(2)}, u32[]{:S(2)}) collective-permute-start(bf16[256,512]{1,0:T(8,128)(2,1)S(1)} %fusion.25), channel_id=1, source_target_pairs={{256,128},{257,129},{258,130},{259,131},{260,132},{261,133},{262,1... | collective-permute-start | bytes 786440 | tf_op jit(solution)/shard_map/ppermute | solution.py:117
  137.6 3.9 %collective-permute-start.3 = (bf16[256,512]{1,0:T(8,128)(2,1)S(1)}, bf16[256,512]{1,0:T(8,128)(2,1)S(1)}, u32[]{:S(2)}, u32[]{:S(2)}) collective-permute-start(bf16[256,512]{1,0:T(8,128)(2,1)S(1)} %get-tuple-element.16), channel_id=1, source_target_pairs={{384,256},{385,257},{386,258},{387,259},{388,260},{389,261},{390,2... | collective-permute-start | bytes 786440 | tf_op jit(solution)/shard_map/ppermute | solution.py:117
  138.2 3.2 %collective-permute-start.6 = (bf16[256,512]{1,0:T(8,128)(2,1)S(1)}, bf16[256,512]{1,0:T(8,128)(2,1)S(1)}, u32[]{:S(2)}, u32[]{:S(2)}) collective-permute-start(bf16[256,512]{1,0:T(8,128)(2,1)S(1)} %get-tuple-element.15), channel_id=1, source_target_pairs={{384,256},{385,257},{386,258},{387,259},{388,260},{389,261},{390,2... | collective-permute-start | bytes 786440 | tf_op jit(solution)/shard_map/ppermute | solution.py:117
  138.9 2.6 collective-permute-start.9
  139.8 60.0 %collective-permute-start.2 = (bf16[256,512]{1,0:T(8,128)(2,1)S(1)}, bf16[256,512]{1,0:T(8,128)(2,1)S(1)}, u32[]{:S(2)}, u32[]{:S(2)}) collective-permute-start(bf16[256,512]{1,0:T(8,128)(2,1)S(1)} %fusion.26), channel_id=1, source_target_pairs={{128,0},{129,1},{130,2},{131,3},{132,4},{133,5},{134,6},{135,7},{1... | collective-permute-start | bytes 786440 | tf_op jit(solution)/shard_map/ppermute | solution.py:117
  141.4 61.4 %copy-start.5 = (f32[512,512,1,1]{1,0,3,2:T(8,128)S(1)}, f32[512,512,1,1]{1,0,3,2:T(8,128)}, u32[]{:S(2)}) copy-start(f32[512,512,1,1]{1,0,3,2:T(8,128)} %copy-done.4) | copy-start | bytes 3145732
  141.5 59.9 %copy-start.10 = (bf16[256,512]{1,0:T(8,128)(2,1)}, bf16[256,512]{1,0:T(8,128)(2,1)S(1)}, u32[]{:S(2)}) copy-start(bf16[256,512]{1,0:T(8,128)(2,1)S(1)} %collective-permute-done.3) | copy-start | bytes 786436
  141.5 59.8 %copy-start.8 = (bf16[256,512]{1,0:T(8,128)(2,1)}, bf16[256,512]{1,0:T(8,128)(2,1)S(1)}, u32[]{:S(2)}) copy-start(bf16[256,512]{1,0:T(8,128)(2,1)S(1)} %collective-permute-done.9) | copy-start | bytes 786436
  201.3 8.6 %copy-start.1 = (f32[256,512]{1,0:T(8,128)S(1)}, f32[256,512]{1,0:T(8,128)}, u32[]{:S(2)}) copy-start(f32[256,512]{1,0:T(8,128)} %copy-done) | copy-start | bytes 1572868
  201.3 8.6 %collective-permute-start.4 = (bf16[256,512]{1,0:T(8,128)(2,1)}, bf16[256,512]{1,0:T(8,128)(2,1)}, u32[]{:S(2)}, u32[]{:S(2)}) collective-permute-start(bf16[256,512]{1,0:T(8,128)(2,1)} %get-tuple-element.10), channel_id=1, source_target_pairs={{256,128},{257,129},{258,130},{259,131},{260,132},{261,133},{262,1... | collective-permute-start | bytes 786440 | tf_op jit(solution)/shard_map/ppermute | solution.py:117
  203.6 24.0 %copy-start.3 = (bf16[4,64,2048]{2,1,0:T(8,128)(2,1)S(1)}, bf16[4,64,2048]{2,1,0:T(8,128)(2,1)}, u32[]{:S(2)}) copy-start(bf16[4,64,2048]{2,1,0:T(8,128)(2,1)} %param.8) | copy-start | bytes 3145732
  203.6 24.0 %copy-start.9 = (bf16[256,512]{1,0:T(8,128)(2,1)S(1)}, bf16[256,512]{1,0:T(8,128)(2,1)}, u32[]{:S(2)}) copy-start(bf16[256,512]{1,0:T(8,128)(2,1)} %copy-done.8) | copy-start | bytes 786436
  203.6 10.2 %all-to-all-start.5 = ((bf16[4,5,16,512]{3,2,1,0:T(8,128)(2,1)}), bf16[4,5,16,512]{3,2,1,0:T(8,128)(2,1)S(1)}, u32[]{:S(2)}, u32[]{:S(2)}) async-start(bf16[4,5,16,512]{3,2,1,0:T(8,128)(2,1)} %maximum_bitcast_fusion), calls=%async_computation.5 | async-start | bytes 655360 | tf_op jit(solution)/shard_map/all_to_all | solution.py:16
  207.2 11.3 %collective-permute-start.10 = (bf16[256,512]{1,0:T(8,128)(2,1)}, bf16[256,512]{1,0:T(8,128)(2,1)}, u32[]{:S(2)}, u32[]{:S(2)}) collective-permute-start(bf16[256,512]{1,0:T(8,128)(2,1)} %get-tuple-element.12), channel_id=1, source_target_pairs={{256,128},{257,129},{258,130},{259,131},{260,132},{261,133},{262,1... | collective-permute-start | bytes 786440 | tf_op jit(solution)/shard_map/ppermute | solution.py:117
  208.6 10.0 %collective-permute-start.7 = (bf16[256,512]{1,0:T(8,128)(2,1)}, bf16[256,512]{1,0:T(8,128)(2,1)}, u32[]{:S(2)}, u32[]{:S(2)}) collective-permute-start(bf16[256,512]{1,0:T(8,128)(2,1)} %get-tuple-element.11), channel_id=1, source_target_pairs={{256,128},{257,129},{258,130},{259,131},{260,132},{261,133},{262,1... | collective-permute-start | bytes 786440 | tf_op jit(solution)/shard_map/ppermute | solution.py:117
  211.9 15.7 %collective-permute-start.5 = (bf16[256,512]{1,0:T(8,128)(2,1)}, bf16[256,512]{1,0:T(8,128)(2,1)}, u32[]{:S(2)}, u32[]{:S(2)}) collective-permute-start(bf16[256,512]{1,0:T(8,128)(2,1)} %fusion.29), channel_id=1, source_target_pairs={{128,0},{129,1},{130,2},{131,3},{132,4},{133,5},{134,6},{135,7},{1... | collective-permute-start | bytes 786440 | tf_op jit(solution)/shard_map/ppermute | solution.py:117
  216.7 16.1 %copy-start.13 = (f32[4,5,16,512]{3,2,1,0:T(8,128)}, f32[4,5,16,512]{3,2,1,0:T(8,128)S(1)}, u32[]{:S(2)}) copy-start(f32[4,5,16,512]{3,2,1,0:T(8,128)S(1)} %convert_element_type.216) | copy-start | bytes 1966084
  218.5 15.2 %copy-start.19 = (f32[1,4,16,512]{3,2,1,0:T(8,128)S(1)}, f32[1,4,16,512]{3,2,1,0:T(8,128)}, u32[]{:S(2)}) copy-start(f32[1,4,16,512]{3,2,1,0:T(8,128)} %param.13) | copy-start | bytes 393220
  230.2 15.5 %collective-permute-start.11 = (bf16[256,512]{1,0:T(8,128)(2,1)}, bf16[256,512]{1,0:T(8,128)(2,1)S(1)}, u32[]{:S(2)}, u32[]{:S(2)}) collective-permute-start(bf16[256,512]{1,0:T(8,128)(2,1)} %get-tuple-element.19), channel_id=1, source_target_pairs={{128,0},{129,1},{130,2},{131,3},{132,4},{133,5},{134,6},{135,7},{1... | collective-permute-start | bytes 786440 | tf_op jit(solution)/shard_map/ppermute | solution.py:117
  231.5 20.0 %collective-permute-start.8 = (bf16[256,512]{1,0:T(8,128)(2,1)}, bf16[256,512]{1,0:T(8,128)(2,1)}, u32[]{:S(2)}, u32[]{:S(2)}) collective-permute-start(bf16[256,512]{1,0:T(8,128)(2,1)} %get-tuple-element.18), channel_id=1, source_target_pairs={{128,0},{129,1},{130,2},{131,3},{132,4},{133,5},{134,6},{135,7},{1... | collective-permute-start | bytes 786440 | tf_op jit(solution)/shard_map/ppermute | solution.py:117
  233.7 19.4 %copy-start.16 = (bf16[256,512]{1,0:T(8,128)(2,1)S(1)}, bf16[256,512]{1,0:T(8,128)(2,1)}, u32[]{:S(2)}) copy-start(bf16[256,512]{1,0:T(8,128)(2,1)} %get-tuple-element.9) | copy-start | bytes 786436
  245.8 0.7 copy-start.21
Sparse Core Ops, SparseCore 0:
  38.7 37.3 all-gather.7
  78.2 53.7 all-gather.5

commit v2 on v1

v2 whole, which is shorter than its diff:
```python
import jax
import jax.numpy as jnp
from jax import lax
from jax.experimental import pallas as pl
from jax.experimental.pallas import tpu as pltpu
from jax.sharding import PartitionSpec as P

EPS = 1e-06

NX = 4
NY = 8
X_GROUPS = [[x * NY + y for x in range(NX)] for y in range(NY)]
Y_GROUPS = [[x * NY + y for y in range(NY)] for x in range(NX)]
CHUNKS = 2
PARAMS = pltpu.CompilerParams(vmem_limit_bytes=40 * 1024 * 1024)


def exchange(block, groups):
    return lax.all_to_all(block, "dp", 0, 0, axis_index_groups=groups, tiled=True)


def spread(block, count, groups):
    return exchange(jnp.broadcast_to(block[None], (count, *block.shape)), groups)


def own_kernel(half, values, near_weight, far_weight, near, far, far_sent):
    rows = values.shape[1]

    def product(weight):
        return jnp.dot(
            values[...],
            weight[...].reshape(rows, weight.shape[-1]),
            preferred_element_type=jnp.float32,
        )

    near[...] = product(near_weight)
    of_far = product(far_weight)
    far[...] = of_far
    far_sent[...] = of_far.astype(jnp.bfloat16)


def own_contribution(half, values, gathered, place, cols):
    tokens, kv = values.shape
    rows_own = kv // (NX * NY)
    result = pl.BlockSpec((tokens, cols), lambda i, h: (0, 0))
    shape = (NY, NX, rows_own, cols)
    return pl.pallas_call(
        own_kernel,
        grid_spec=pltpu.PrefetchScalarGridSpec(
            num_scalar_prefetch=1,
            grid=(1,),
            in_specs=[
                pl.BlockSpec((tokens, kv), lambda i, h: (0, 0)),
                pl.BlockSpec(shape, lambda i, h: (0, 0, h[0], place)),
                pl.BlockSpec(shape, lambda i, h: (0, 0, 1 - h[0], place)),
            ],
            out_specs=[result, result, result],
        ),
        out_shape=[
            jax.ShapeDtypeStruct((tokens, cols), jnp.float32),
            jax.ShapeDtypeStruct((tokens, cols), jnp.float32),
            jax.ShapeDtypeStruct((tokens, cols), jnp.bfloat16),
        ],
        cost_estimate=pl.CostEstimate(
            flops=4 * tokens * kv * cols, bytes_accessed=3 * 1024 * 1024, transcendentals=0
        ),
        compiler_params=PARAMS,
    )(half.reshape(1).astype(jnp.int32), values, gathered, gathered)


def solve_kernel(y_ref, stats, block, sent, rows, left, right, matrix):
    own = stats.shape[2]
    size = block.shape[-1]
    y = y_ref[0]
    for x in range(NX):
        for other in range(NY):
            place = slice((x * NY + other) * own, (x * NY + other + 1) * own)
            rows[place, :] = block[other, x]
            left[place, :] = stats[other, x, :, :size].astype(jnp.float32)
            right[place, :] = stats[other, x, :, size:].astype(jnp.float32)
    whole = rows[...]
    starts = [pl.multiple_of(x * NY * own + y * own, own) for x in range(NX)]

    def mine(ref):
        return jnp.concatenate([ref[pl.ds(start, own), :] for start in starts], axis=0)

    picked = mine(rows)
    for x in range(NX):
        sent[x, 0] = picked[x * own : (x + 1) * own]
    line = lax.broadcasted_iota(jnp.int32, (NX * own, size), 0)
    line = (line // own) * (NY * own) + y * own + line % own
    column = lax.broadcasted_iota(jnp.int32, (NX * own, size), 1)
    identity = jnp.where(line == column, 1.0, 0.0)
    for side, (ref, dims) in enumerate(((left, 1), (right, 0))):
        gram = lax.dot_general(
            whole, whole, (((dims,), (dims,)), ((), ())), preferred_element_type=jnp.float32
        )
        stat = ref[...] + gram
        ref[...] = stat
        now = mine(ref)
        total = jnp.sum(stat * stat, axis=1, keepdims=True)
        total = jnp.sum(total, axis=0, keepdims=True) / (size * size)
        scale = 1.0 / (jnp.sqrt(total + EPS) * size)
        matrix[...] = (stat * scale).astype(jnp.bfloat16)
        first = now * scale
        term = first
        for _ in range(5):
            term = 1.25 * term - 0.25 * jnp.dot(
                term.astype(jnp.bfloat16), matrix[...], preferred_element_type=jnp.float32
            )
        root = 0.25 * (6.25 * identity - 1.25 * first - term)
        root = root.astype(jnp.bfloat16)
        ref[...] = gram
        gram_rows = mine(ref).astype(jnp.bfloat16)
        for x in range(NX):
            part = slice(x * own, (x + 1) * own)
            sent[x, 1 + side] = gram_rows[part]
            sent[x, 3 + side] = root[part]


def solve(y_index, gathered, block):
    own, size = block.shape[2:]
    return pl.pallas_call(
        solve_kernel,
        grid=(1,),
        in_specs=[
            pl.BlockSpec(memory_space=pltpu.SMEM),
            pl.BlockSpec((NY, NX, own, 2 * size), lambda i: (0, 0, 2, 0)),
            pl.BlockSpec(block.shape, lambda i: (0, 0, 0, 0)),
        ],
        out_specs=pl.BlockSpec((NX, 5, own, size), lambda i: (0, 0, 0, 0)),
        out_shape=jax.ShapeDtypeStruct((NX, 5, own, size), jnp.bfloat16),
        scratch_shapes=[
            pltpu.VMEM((size, size), jnp.bfloat16),
            pltpu.VMEM((size, size), jnp.float32),
            pltpu.VMEM((size, size), jnp.float32),
            pltpu.VMEM((size, size), jnp.bfloat16),
        ],
        cost_estimate=pl.CostEstimate(
            flops=3 * 2 * size**3, bytes_accessed=2 * 1024 * 1024, transcendentals=0
        ),
        compiler_params=PARAMS,
    )(y_index.reshape(1).astype(jnp.int32), gathered, block)


def finish_kernel(refresh, back, left_stats, right_stats, weight_grad, new_left, new_right, roots):
    size = back.shape[-1]
    for b in range(NX):
        weight_grad[:, b * size : (b + 1) * size] = back[b, 0].astype(jnp.float32)
        new_left[b] = left_stats[b] + back[b, 1].astype(jnp.float32)
        new_right[b] = right_stats[b] + back[b, 2].astype(jnp.float32)
    for k in range(roots.shape[0] // 2):
        chosen = refresh[k]
        roots[2 * k] = back[chosen, 3].astype(jnp.float32)
        roots[2 * k + 1] = back[chosen, 4].astype(jnp.float32)


def finish(refresh, back, left_stats, right_stats):
    own, size = back.shape[2:]
    picks = 2 * refresh.shape[0]
    shapes = [
        (own, NX * size),
        left_stats.shape,
        right_stats.shape,
        (picks, own, size),
    ]
    vmem = pl.BlockSpec(memory_space=pltpu.VMEM)
    return pl.pallas_call(
        finish_kernel,
        in_specs=[pl.BlockSpec(memory_space=pltpu.SMEM), vmem, vmem, vmem],
        out_specs=[vmem] * 4,
        out_shape=[jax.ShapeDtypeStruct(s, jnp.float32) for s in shapes],
        cost_estimate=pl.CostEstimate(
            flops=1024, bytes_accessed=2 * 1024 * 1024, transcendentals=0
        ),
        compiler_params=PARAMS,
    )(refresh, back, left_stats, right_stats)


def per_device(top_grad, stash, value_grad, value_weight, left_stats, right_stats, refresh, order):
    micro, tok_dev, width = top_grad.shape
    rows_own = value_weight.shape[1]
    blocks = left_stats.shape[1]
    kv = left_stats.shape[3]
    tokens = micro * tok_dev
    section = lax.axis_index("section")
    y_index = lax.axis_index("dp") % NY

    value_full = lax.all_gather(value_grad[0], "tensor", axis=2, tiled=True)

    stats = jnp.concatenate([left_stats[0], right_stats[0]], axis=2).astype(jnp.bfloat16)
    halves = value_weight[0].reshape(rows_own, 2, width // 2).transpose(1, 0, 2)
    halves = jnp.broadcast_to(halves.reshape(1, -1, width // 2), (NX, 2 * rows_own, width // 2))
    first = exchange(jnp.concatenate([halves, stats], axis=1), X_GROUPS)
    gathered = lax.all_gather(first, "dp", axis=0, axis_index_groups=Y_GROUPS)

    paired = jnp.take(value_full, order, axis=0).reshape(tokens, kv)
    inputs = stash[0].reshape(tokens, width)
    partial = jnp.stack(
        [
            lax.dot_general(
                paired,
                inputs[:, b * kv : (b + 1) * kv],
                (((0,), (0,)), ((), ())),
                preferred_element_type=jnp.float32,
            ).astype(jnp.bfloat16)
            for b in range(blocks)
        ]
    )
    over_x = exchange(partial, X_GROUPS)
    over_x = jnp.sum(over_x.astype(jnp.float32), axis=0).astype(jnp.bfloat16)
    by_y = over_x.reshape(NX, NY, rows_own, kv).transpose(1, 0, 2, 3)
    over_y = exchange(by_y, Y_GROUPS)

    value_own = value_full.reshape(tokens, NX, NY, rows_own).transpose(0, 2, 1, 3)
    value_own = value_own.reshape(tokens, kv)
    is_left = (section == 1) | (section == 2)
    cols = width // 2 // CHUNKS
    owns = [
        own_contribution(jnp.where(is_left, 0, 1), value_own, gathered, k, cols)
        for k in range(CHUNKS)
    ]
    over_y, _ = lax.optimization_barrier((over_y, owns))
    own = jnp.sum(over_y.astype(jnp.float32), axis=0)
    block = spread(own.astype(jnp.bfloat16), NY, Y_GROUPS)

    top = top_grad.reshape(tokens, 2, width // 2)
    top_near = jnp.where(is_left, top[:, 0], top[:, 1])
    top_far = jnp.where(is_left, top[:, 1], top[:, 0])
    f32, bf16 = jnp.float32, jnp.bfloat16
    mates = [lax.ppermute(sent, "section", [(3, 2), (2, 3), (1, 0)]) for _, _, sent in owns]
    helds, bases, seconds = [], [], []
    for k, (near, _, _) in enumerate(owns):
        mate = mates[k]
        if k:
            mate, _ = lax.optimization_barrier((mate, helds[-1]))
        base = near + mate.astype(f32)
        bases.append(base)
        helds.append((top_near[:, k * cols : (k + 1) * cols].astype(f32) + base).astype(bf16))
        seconds.append(lax.ppermute(helds[-1], "section", [(2, 1), (3, 0)]))
    nears, fars = [], []
    last = helds[-1]
    for k, (near, far, _) in enumerate(owns):
        part = slice(k * cols, (k + 1) * cols)
        second, _ = lax.optimization_barrier((seconds[k], last))
        updated = (second.astype(f32) + bases[k]).astype(bf16)
        alone = (top_near[:, part].astype(f32) + near).astype(bf16)
        passed = jnp.where(section == 0, second, jnp.where(section == 1, updated, helds[k]))
        last = passed
        nears.append(
            jnp.where(section == 3, alone, jnp.where(section == 2, helds[k], updated))
        )
        third = lax.ppermute(passed, "section", [(1, 0), (0, 1), (3, 2)])
        fars.append((third, far, top_far[:, part]))

    block, _ = lax.optimization_barrier((block, helds))
    sent = solve(y_index, gathered, block)
    fars, _ = lax.optimization_barrier((fars, sent))
    back = exchange(sent, X_GROUPS)
    weight_grad, new_left, new_right, roots = finish(
        refresh[0, 0], back, left_stats[0], right_stats[0]
    )
    fars = [
        jnp.where(
            section == 2,
            third,
            (jnp.where(section == 3, above, third).astype(f32) + far).astype(bf16),
        )
        for third, far, above in fars
    ]
    near, far = jnp.concatenate(nears, axis=1), jnp.concatenate(fars, axis=1)
    section_grad = jnp.concatenate(
        [jnp.where(is_left, near, far), jnp.where(is_left, far, near)], axis=1
    ).reshape(micro, tok_dev, width)
    return (
        section_grad[None],
        weight_grad[None],
        new_left[None],
        new_right[None],
        roots[None, None],
    )


def solution(mesh):
    return jax.shard_map(
        per_device,
        mesh=mesh,
        in_specs=(
            P(None, "dp", "tensor"),
            P("section", None, "dp", "tensor"),
            P("section", None, "dp", "tensor"),
            P("section", "dp", "tensor"),
            P("section", "tensor", "dp", None),
            P("section", "tensor", "dp", None),
            P("section", "tensor", None),
            P(),
        ),
        out_specs=(
            P("section", None, "dp", "tensor"),
            P("section", "dp", "tensor"),
            P("section", "tensor", "dp", None),
            P("section", "tensor", "dp", None),
            P("section", "tensor", None, "dp", None),
        ),
        check_vma=False,
    )
```

time: 262 us -> 171 us (0.65)
  the two profiles are of different devices: /device:TPU:1 before, /device:TPU:8 now
where the time goes in v2:
time: 171 us; the launch traced here: 170 us
  waiting for transfers between devices  53.6 us (31%)
  starting transfers between devices  47.1 us (28%)
  blocking collectives  18.9 us (11%)
  between operations  14.5 us (8%)
  other arithmetic  14.4 us (8%)
  local copies, waits for them, and re-layouts  13.5 us (8%)
  Pallas kernels  7.1 us (4%)
    all_to_all x4, waiting for transfers between devices, exchange(): lax.all_to_all(block, 'dp', 0, 0, axis_index_groups=groups, tiled=True)  24.4 us
    ppermute x2, waiting for transfers between devices, per_device(): lax.ppermute(sent, 'section', [(3, 2), (2, 3), (1, 0)])  23.6 us
    all_to_all x4, starting transfers between devices, exchange(): lax.all_to_all(block, 'dp', 0, 0, axis_index_groups=groups, tiled=True)  21.9 us
    ppermute x2, starting transfers between devices, per_device(): third = lax.ppermute(passed, 'section', [(1, 0), (0, 1), (3, 2)])  19.6 us
    all_to_all x1, blocking collectives, exchange(): lax.all_to_all(block, 'dp', 0, 0, axis_index_groups=groups, tiled=True)  12.3 us
    all_gather x1, blocking collectives, per_device(): value_full = lax.all_gather(value_grad[0], 'tensor', axis=2, tiled=True)  6.63 us
    ppermute x2, waiting for transfers between devices, per_device(): third = lax.ppermute(passed, 'section', [(1, 0), (0, 1), (3, 2)])  5.61 us
    pallas_call x1, Pallas kernels, solve(): pl.pallas_call(solve_kernel, grid=(1,), in_specs=[pl.BlockSpec(memory_spa...  4.86 us
  transfers between devices with their start and end apart: 11, of which 3 were waited for; matrix products, arithmetic and copies ran while one was open for 13% of the time, Pallas kernels for 3%

profile of v2, /device:TPU:8, one launch (start us, length us, event | category | flops | bytes accessed | tf_op | source)
XLA Modules:
  0.0 170.5 jit_solution(13586943400224626244)
XLA Ops:
  7.2 0.9 reshape_squeeze.6
  8.1 1.0 bitcast_convert_fusion.1
  9.1 0.9 bitcast_convert_fusion
  10.1 12.3 %all_to_all.25 = bf16[4,48,1024]{2,1,0:T(8,128)(2,1)} all-to-all(bf16[4,48,1024]{2,1,0:T(8,128)(2,1)S(1)} %maximum_maximum_fusion), channel_id=1, replica_groups={{0,32,64,96},{4,36,68,100},{8,40,72,104},{12,44,76,108},{16,48,80,112},..., dimensions={0} | all-to-all | bytes 786432 | tf_op jit(solution)/shard_map/all_to_all | solution.py:19
  22.6 6.6 %all-gather = bf16[1,4,64,512]{3,2,1,0:T(8,128)(2,1)S(1)} all-gather(bf16[1,4,64,128]{3,2,1,0:T(8,128)(2,1)S(1)} %copy-done.17), channel_id=2, replica_groups=mesh['section'=4,'dp'=32,'tensor'=4] {'tensor'}, dimensions={3}, use_global_device_ids=true | all-gather | bytes 327680 | tf_op jit(solution)/shard_map/all_gather | solution.py:189
  29.3 0.6 gather_fusion
  29.9 0.3 fusion.3
  30.3 0.3 fusion.2
  30.6 0.3 fusion.1
  31.0 0.3 fusion
  31.3 1.6 pad_maximum_fusion
  32.9 3.6 %all-to-all-start.1 = ((bf16[4,512,512]{2,1,0:T(8,128)(2,1)}), bf16[4,512,512]{2,1,0:T(8,128)(2,1)S(1)}, u32[]{:S(2)}, u32[]{:S(2)}) async-start(bf16[4,512,512]{2,1,0:T(8,128)(2,1)} %pad_maximum_fusion), calls=%async_computation.1 | async-start | bytes 4194304 | tf_op jit(solution)/shard_map/all_to_all | solution.py:19
  36.5 0.3 copy.36
  36.8 0.3 reshape.158
  37.3 1.8 %reshape.156 = bf16[256,2,1024]{2,1,0:T(2,128)(2,1)S(1)} reshape(bf16[4,64,2048]{2,1,0:T(8,128)(2,1)} %param.8) | data formatting | bytes 2097152 | tf_op jit(solution)/shard_map/reshape | solution.py:227
  39.2 24.4 %all-to-all-done.1 = bf16[4,512,512]{2,1,0:T(8,128)(2,1)S(1)} async-done(((bf16[4,512,512]{2,1,0:T(8,128)(2,1)}), bf16[4,512,512]{2,1,0:T(8,128)(2,1)S(1)}, u32[]{:S(2)}, u32[]{:S(2)}) %all-to-all-start.1) | async-done | bytes 2097184 | tf_op jit(solution)/shard_map/all_to_all | solution.py:19
  63.6 1.2 reduce_sum.24
  64.8 1.9 %copy.41 = bf16[8,4,16,512]{3,2,1,0:T(8,128)(2,1)} copy(bf16[8,4,16,512]{3,2,0,1:T(8,128)(2,1)} %bitcast.54) | data formatting | bytes 1048576 | tf_op jit(solution)/shard_map/transpose | solution.py:212
  66.7 7.5 %all-to-all-start.2 = ((bf16[8,4,16,512]{3,2,1,0:T(8,128)(2,1)}), bf16[8,4,16,512]{3,2,1,0:T(8,128)(2,1)}, u32[]{:S(2)}, u32[]{:S(2)}) async-start(bf16[8,4,16,512]{3,2,1,0:T(8,128)(2,1)} %copy.41), calls=%async_computation.2 | async-start | bytes 1048576 | tf_op jit(solution)/shard_map/all_to_all | solution.py:19
  74.3 2.3 %fusion.16 = (bf16[256,1,1024]{2,1,0:T(2,128)(2,1)S(1)}, bf16[256,1,1024]{2,1,0:T(2,128)(2,1)}) fusion(bf16[256,2,1024]{2,1,0:T(2,128)(2,1)S(1)} %reshape.156), kind=kLoop, calls=%fused_computation.48 | loop fusion | bytes 2097152 | tf_op jit(solution)/shard_map/slice | solution.py:228
  76.5 1.9 %copy-done = bf16[32,48,1024]{2,1,0:T(8,128)(2,1)S(1)} copy-done((bf16[32,48,1024]{2,1,0:T(8,128)(2,1)S(1)}, bf16[32,48,1024]{2,1,0:T(8,128)(2,1)}, u32[]{:S(2)}) %copy-start) | copy-done | bytes 3145752
  78.4 0.4 shard_map.120
  78.9 0.8 copy-done.4
  79.7 1.4 collective-permute-start.2
  81.1 0.4 shard_map.119
  81.5 1.3 collective-permute-start
  82.8 1.1 select_bitcast_fusion
  84.0 23.6 %collective-permute-done = bf16[256,512]{1,0:T(8,128)(2,1)S(1)} collective-permute-done((bf16[256,512]{1,0:T(8,128)(2,1)S(1)}, bf16[256,512]{1,0:T(8,128)(2,1)S(1)}, u32[]{:S(2)}, u32[]{:S(2)}) %collective-permute-start) | collective-permute-done | bytes 262176 | tf_op jit(solution)/shard_map/ppermute | solution.py:231
  107.5 0.7 copy-done.13
  108.4 1.4 collective-permute-start.1
  109.8 1.1 reduce_sum.25
  111.0 0.9 broadcast_in_dim.48
  111.8 7.2 %all-to-all-start.3 = ((bf16[8,4,16,512]{3,2,1,0:T(8,128)(2,1)}), bf16[8,4,16,512]{3,2,1,0:T(8,128)(2,1)}, u32[]{:S(2)}, u32[]{:S(2)}) async-start(bf16[8,4,16,512]{3,2,1,0:T(8,128)(2,1)} %broadcast_in_dim.48), calls=%async_computation.3 | async-start | bytes 1048576 | tf_op jit(solution)/shard_map/all_to_all | solution.py:19
  119.2 1.4 collective-permute-start.3
  120.6 0.9 fusion.11
  121.5 0.7 select_select_fusion.1
  122.3 16.8 %collective-permute-start.4 = (bf16[256,512]{1,0:T(8,128)(2,1)}, bf16[256,512]{1,0:T(8,128)(2,1)}, u32[]{:S(2)}, u32[]{:S(2)}) collective-permute-start(bf16[256,512]{1,0:T(8,128)(2,1)} %select_select_fusion.1), channel_id=1, source_target_pairs={{128,0},{0,128},{384,256},{129,1},{1,129},{385,257},{130,2},{2,130... | collective-permute-start | bytes 786440 | tf_op jit(solution)/shard_map/ppermute | solution.py:253
  139.1 1.9 %fusion.10 = (bf16[256,512]{1,0:T(8,128)(2,1)}, bf16[256,512]{1,0:T(8,128)(2,1)S(1)}) fusion(f32[256,512]{1,0:T(8,128)S(1)} %copy-done.3, bf16[256,512]{1,0:T(8,128)(2,1)S(1)} %fusion.6, pred[]{:T(512)S(6)} %eq.11, pred[]{:T(512)S(6)} %eq.12, bf16[256,1024]{1,0:T(8,128)(2,1)} %copy-done.9, bf16[256,512]{1,0:T(8,128)(2,1)S(1)} %collective-permute-done.2, ...), kind=kLoop, calls=%fused_computation.34 | loop fusion | flops 1310720 | bytes 2097154 | tf_op jit(solution)/shard_map/jit(_where)/select_n | solution.py:251
  141.0 0.7 select_select_fusion
  141.7 2.8 %collective-permute-start.5 = (bf16[256,512]{1,0:T(8,128)(2,1)}, bf16[256,512]{1,0:T(8,128)(2,1)}, u32[]{:S(2)}, u32[]{:S(2)}) collective-permute-start(bf16[256,512]{1,0:T(8,128)(2,1)} %select_select_fusion), channel_id=1, source_target_pairs={{128,0},{0,128},{384,256},{129,1},{1,129},{385,257},{130,2},{2,130... | collective-permute-start | bytes 786440 | tf_op jit(solution)/shard_map/ppermute | solution.py:253
  144.5 0.7 fusion.17
  145.3 4.9 %shard_map.121 = bf16[4,5,16,512]{3,2,1,0:T(8,128)(2,1)} custom-call(s32[1]{0:T(128)} %bitcast.12.y_ref, bf16[8,4,48,1024]{3,2,1,0:T(8,128)(2,1)S(1)} %bitcast.49, bf16[8,4,16,512]{3,2,1,0:T(8,128)(2,1)} %all-to-all-done.3.block), custom_call_target="tpu_custom_call" | custom-call | flops 805306368 | bytes 2097152 | tf_op jit(solution)/shard_map/pallas_call | solution.py:123
  150.1 3.6 %all-to-all-start.4 = ((bf16[4,5,16,512]{3,2,1,0:T(8,128)(2,1)}), bf16[4,5,16,512]{3,2,1,0:T(8,128)(2,1)S(1)}, u32[]{:S(2)}, u32[]{:S(2)}) async-start(bf16[4,5,16,512]{3,2,1,0:T(8,128)(2,1)} %shard_map.121), calls=%async_computation.4 | async-start | bytes 655360 | tf_op jit(solution)/shard_map/all_to_all | solution.py:19
  153.7 5.6 %collective-permute-done.5 = bf16[256,512]{1,0:T(8,128)(2,1)} collective-permute-done((bf16[256,512]{1,0:T(8,128)(2,1)}, bf16[256,512]{1,0:T(8,128)(2,1)}, u32[]{:S(2)}, u32[]{:S(2)}) %collective-permute-start.5) | collective-permute-done | bytes 262176 | tf_op jit(solution)/shard_map/ppermute | solution.py:253
  159.3 1.6 fusion.8
  161.0 0.2 broadcast_select_fusion.1
  161.2 1.1 pad_maximum_fusion.1
  162.3 1.4 shard_map.122
  (58 shorter events, 0.9 us)
Async XLA Ops:
  7.2 15.3 %copy-start.18 = (s32[4]{0:T(128)S(1)}, s32[4]{0:T(128)}, u32[]{:S(2)}) copy-start(s32[4]{0:T(128)} %param.15) | copy-start | bytes 52
  7.2 15.4 %copy-start.17 = (bf16[1,4,64,128]{3,2,1,0:T(8,128)(2,1)S(1)}, bf16[1,4,64,128]{3,2,1,0:T(8,128)(2,1)}, u32[]{:S(2)}) copy-start(bf16[1,4,64,128]{3,2,1,0:T(8,128)(2,1)} %param.10) | copy-start | bytes 196612
  7.2 69.3 %all-gather.4.cloned.1.call-start = ((), (), s32[]{:S(2)}) async-start(), calls=%async_computation.5 | async-start | bytes 3538944 | tf_op jit(solution)/shard_map/all_gather | solution.py:195
  8.1 21.8 %copy-start.12 = (bf16[1,4,64,2048]{3,2,1,0:T(8,128)(2,1)S(1)}, bf16[1,4,64,2048]{3,2,1,0:T(8,128)(2,1)}, u32[]{:S(2)}) copy-start(bf16[1,4,64,2048]{3,2,1,0:T(8,128)(2,1)} %param.9) | copy-start | bytes 3145732
  32.9 30.7 %all-to-all-start.1 = ((bf16[4,512,512]{2,1,0:T(8,128)(2,1)}), bf16[4,512,512]{2,1,0:T(8,128)(2,1)S(1)}, u32[]{:S(2)}, u32[]{:S(2)}) async-start(bf16[4,512,512]{2,1,0:T(8,128)(2,1)} %pad_maximum_fusion), calls=%async_computation.1 | async-start | bytes 4194304 | tf_op jit(solution)/shard_map/all_to_all | solution.py:19
  66.7 43.1 %all-to-all-start.2 = ((bf16[8,4,16,512]{3,2,1,0:T(8,128)(2,1)}), bf16[8,4,16,512]{3,2,1,0:T(8,128)(2,1)}, u32[]{:S(2)}, u32[]{:S(2)}) async-start(bf16[8,4,16,512]{3,2,1,0:T(8,128)(2,1)} %copy.41), calls=%async_computation.2 | async-start | bytes 1048576 | tf_op jit(solution)/shard_map/all_to_all | solution.py:19
  76.5 1.9 %copy-start = (bf16[32,48,1024]{2,1,0:T(8,128)(2,1)S(1)}, bf16[32,48,1024]{2,1,0:T(8,128)(2,1)}, u32[]{:S(2)}) copy-start(bf16[32,48,1024]{2,1,0:T(8,128)(2,1)} %all-gather.4.cloned.1.call-done) | copy-start | bytes 9437188
  78.9 0.8 copy-start.4
  79.7 39.4 %copy-start.2 = (f32[256,512]{1,0:T(8,128)}, f32[256,512]{1,0:T(8,128)S(1)}, u32[]{:S(2)}) copy-start(f32[256,512]{1,0:T(8,128)S(1)} %get-tuple-element.28) | copy-start | bytes 1572868
  79.7 3.2 %copy-start.10 = (bf16[256,1,1024]{2,1,0:T(2,128)(2,1)S(1)}, bf16[256,1,1024]{2,1,0:T(2,128)(2,1)}, u32[]{:S(2)}) copy-start(bf16[256,1,1024]{2,1,0:T(2,128)(2,1)} %get-tuple-element.56) | copy-start | bytes 1572868
  79.7 39.4 %collective-permute-start.2 = (bf16[256,512]{1,0:T(8,128)(2,1)S(1)}, bf16[256,512]{1,0:T(8,128)(2,1)S(1)}, u32[]{:S(2)}, u32[]{:S(2)}) collective-permute-start(bf16[256,512]{1,0:T(8,128)(2,1)S(1)} %get-tuple-element.29), channel_id=1, source_target_pairs={{384,256},{256,384},{128,0},{385,257},{257,385},{129,1},{386,258},... | collective-permute-start | bytes 786440 | tf_op jit(solution)/shard_map/ppermute | solution.py:231
  81.5 26.8 %copy-start.5 = (f32[256,512]{1,0:T(8,128)}, f32[256,512]{1,0:T(8,128)S(1)}, u32[]{:S(2)}) copy-start(f32[256,512]{1,0:T(8,128)S(1)} %get-tuple-element.39) | copy-start | bytes 1572868
  81.5 26.0 %collective-permute-start = (bf16[256,512]{1,0:T(8,128)(2,1)S(1)}, bf16[256,512]{1,0:T(8,128)(2,1)S(1)}, u32[]{:S(2)}, u32[]{:S(2)}) collective-permute-start(bf16[256,512]{1,0:T(8,128)(2,1)S(1)} %get-tuple-element.27), channel_id=1, source_target_pairs={{384,256},{256,384},{128,0},{385,257},{257,385},{129,1},{386,258},... | collective-permute-start | bytes 786440 | tf_op jit(solution)/shard_map/ppermute | solution.py:231
  83.9 37.6 %copy-start.9 = (bf16[256,1024]{1,0:T(8,128)(2,1)}, bf16[256,1024]{1,0:T(8,128)(2,1)S(1)}, u32[]{:S(2)}) copy-start(bf16[256,1024]{1,0:T(8,128)(2,1)S(1)} %get-tuple-element.52) | copy-start | bytes 1572868
  107.5 0.7 copy-start.13
  108.4 12.2 %copy-start.14 = (bf16[256,512]{1,0:T(8,128)(2,1)S(1)}, bf16[256,512]{1,0:T(8,128)(2,1)}, u32[]{:S(2)}) copy-start(bf16[256,512]{1,0:T(8,128)(2,1)} %copy-done.13) | copy-start | bytes 786436
  108.4 12.2 %collective-permute-start.1 = (bf16[256,512]{1,0:T(8,128)(2,1)S(1)}, bf16[256,512]{1,0:T(8,128)(2,1)S(1)}, u32[]{:S(2)}, u32[]{:S(2)}) collective-permute-start(bf16[256,512]{1,0:T(8,128)(2,1)S(1)} %fusion.5), channel_id=1, source_target_pairs={{256,128},{384,0},{257,129},{385,1},{258,130},{386,2},{259,131},{3... | collective-permute-start | bytes 786440 | tf_op jit(solution)/shard_map/ppermute | solution.py:240
  111.8 33.4 %all-to-all-start.3 = ((bf16[8,4,16,512]{3,2,1,0:T(8,128)(2,1)}), bf16[8,4,16,512]{3,2,1,0:T(8,128)(2,1)}, u32[]{:S(2)}, u32[]{:S(2)}) async-start(bf16[8,4,16,512]{3,2,1,0:T(8,128)(2,1)} %broadcast_in_dim.48), calls=%async_computation.3 | async-start | bytes 1048576 | tf_op jit(solution)/shard_map/all_to_all | solution.py:19
  119.2 20.0 %copy-start.3 = (f32[256,512]{1,0:T(8,128)S(1)}, f32[256,512]{1,0:T(8,128)}, u32[]{:S(2)}) copy-start(f32[256,512]{1,0:T(8,128)} %copy-done.2) | copy-start | bytes 1572868
  119.2 19.9 %collective-permute-start.3 = (bf16[256,512]{1,0:T(8,128)(2,1)S(1)}, bf16[256,512]{1,0:T(8,128)(2,1)S(1)}, u32[]{:S(2)}, u32[]{:S(2)}) collective-permute-start(bf16[256,512]{1,0:T(8,128)(2,1)S(1)} %fusion.6), channel_id=1, source_target_pairs={{256,128},{384,0},{257,129},{385,1},{258,130},{386,2},{259,131},{3... | collective-permute-start | bytes 786440 | tf_op jit(solution)/shard_map/ppermute | solution.py:240
  121.5 23.0 %copy-start.11 = (bf16[256,1024]{1,0:T(8,128)(2,1)S(1)}, bf16[256,1024]{1,0:T(8,128)(2,1)}, u32[]{:S(2)}) copy-start(bf16[256,1024]{1,0:T(8,128)(2,1)} %get-tuple-element.51) | copy-start | bytes 1572868
  122.3 23.0 %copy-start.1 = (bf16[32,48,1024]{2,1,0:T(8,128)(2,1)S(1)}, bf16[32,48,1024]{2,1,0:T(8,128)(2,1)}, u32[]{:S(2)}) copy-start(bf16[32,48,1024]{2,1,0:T(8,128)(2,1)} %all-gather.4.cloned.1.call-done) | copy-start | bytes 9437188
  122.3 37.1 %collective-permute-start.4 = (bf16[256,512]{1,0:T(8,128)(2,1)}, bf16[256,512]{1,0:T(8,128)(2,1)}, u32[]{:S(2)}, u32[]{:S(2)}) collective-permute-start(bf16[256,512]{1,0:T(8,128)(2,1)} %select_select_fusion.1), channel_id=1, source_target_pairs={{128,0},{0,128},{384,256},{129,1},{1,129},{385,257},{130,2},{2,130... | collective-permute-start | bytes 786440 | tf_op jit(solution)/shard_map/ppermute | solution.py:253
  141.7 17.6 %collective-permute-start.5 = (bf16[256,512]{1,0:T(8,128)(2,1)}, bf16[256,512]{1,0:T(8,128)(2,1)}, u32[]{:S(2)}, u32[]{:S(2)}) collective-permute-start(bf16[256,512]{1,0:T(8,128)(2,1)} %select_select_fusion), channel_id=1, source_target_pairs={{128,0},{0,128},{384,256},{129,1},{1,129},{385,257},{130,2},{2,130... | collective-permute-start | bytes 786440 | tf_op jit(solution)/shard_map/ppermute | solution.py:253
  150.1 10.8 %copy-start.15 = (bf16[256,512]{1,0:T(8,128)(2,1)S(1)}, bf16[256,512]{1,0:T(8,128)(2,1)}, u32[]{:S(2)}) copy-start(bf16[256,512]{1,0:T(8,128)(2,1)} %get-tuple-element.47) | copy-start | bytes 786436
  150.1 10.8 %copy-start.16 = (bf16[256,512]{1,0:T(8,128)(2,1)S(1)}, bf16[256,512]{1,0:T(8,128)(2,1)}, u32[]{:S(2)}) copy-start(bf16[256,512]{1,0:T(8,128)(2,1)} %get-tuple-element.49) | copy-start | bytes 786436
  150.1 12.1 %all-to-all-start.4 = ((bf16[4,5,16,512]{3,2,1,0:T(8,128)(2,1)}), bf16[4,5,16,512]{3,2,1,0:T(8,128)(2,1)S(1)}, u32[]{:S(2)}, u32[]{:S(2)}) async-start(bf16[4,5,16,512]{3,2,1,0:T(8,128)(2,1)} %shard_map.121), calls=%async_computation.4 | async-start | bytes 655360 | tf_op jit(solution)/shard_map/all_to_all | solution.py:19
  160.9 1.3 copy-start.6
  161.0 1.3 copy-start.7
  161.0 1.3 copy-start.8
Sparse Core Ops, SparseCore 0:
  22.5 49.9 all-gather.3

commit v3 on v2

--- a/solution.py
+++ b/solution.py
@@ -11,7 +11,8 @@
 NY = 8
 X_GROUPS = [[x * NY + y for x in range(NX)] for y in range(NY)]
 Y_GROUPS = [[x * NY + y for y in range(NY)] for x in range(NX)]
-CHUNKS = 2
+PIECE = 256
+SPLIT = 3
 PARAMS = pltpu.CompilerParams(vmem_limit_bytes=40 * 1024 * 1024)
 
 
@@ -19,65 +20,135 @@
     return lax.all_to_all(block, "dp", 0, 0, axis_index_groups=groups, tiled=True)
 
 
-def spread(block, count, groups):
-    return exchange(jnp.broadcast_to(block[None], (count, *block.shape)), groups)
-
-
-def own_kernel(half, values, near_weight, far_weight, near, far, far_sent):
+def pack_kernel(weight, left, right, packed):
+    own = weight.shape[0]
+    per_half = weight.shape[1] // (2 * PIECE)
+    rest = per_half - SPLIT
+
+    def put(x, group, piece):
+        packed[x, group * own : (group + 1) * own, :] = piece
+
+    for h in range(2):
+        for p in range(per_half):
+            group = h * SPLIT + p if p < SPLIT else 2 * SPLIT + h * rest + p - SPLIT
+            column = (h * per_half + p) * PIECE
+            for x in range(NX):
+                put(x, group, weight[:, column : column + PIECE])
+    group = 2 * per_half
+    for ref in (left, right):
+        for p in range(ref.shape[2] // PIECE):
+            for x in range(NX):
+                put(x, group, ref[x, :, p * PIECE : (p + 1) * PIECE].astype(jnp.bfloat16))
+            group += 1
+
+
+def pack(weight, left, right):
+    own, width = weight.shape
+    rows = own * (width + 2 * left.shape[2]) // PIECE
+    return whole_call(
+        pack_kernel, jax.ShapeDtypeStruct((NX, rows, PIECE), jnp.bfloat16), weight, left, right
+    )
+
+
+def over_x_kernel(parts, result):
+    own = result.shape[2]
+    for x in range(NX):
+        for y in range(NY):
+            place = slice((x * NY + y) * own, (x * NY + y + 1) * own)
+            total = parts[0, place, :].astype(jnp.float32)
+            for k in range(1, NX):
+                total += parts[k, place, :].astype(jnp.float32)
+            result[y, x] = total.astype(jnp.bfloat16)
+
+
+def over_y_kernel(parts, result):
+    total = parts[0].astype(jnp.float32)
+    for k in range(1, NY):
+        total += parts[k].astype(jnp.float32)
+    total = total.astype(jnp.bfloat16)
+    for k in range(NY):
+        result[k] = total
+
+
+def whole_call(kernel, out_shape, *operands):
+    vmem = pl.BlockSpec(memory_space=pltpu.VMEM)
+    return pl.pallas_call(
+        kernel,
+        in_specs=[vmem] * len(operands),
+        out_specs=vmem,
+        out_shape=out_shape,
+        cost_estimate=pl.CostEstimate(
+            flops=1024, bytes_accessed=2 * 1024 * 1024, transcendentals=0
+        ),
+        compiler_params=PARAMS,
+    )(*operands)
+
+
+def own_kernel(half, values, *refs):
     rows = values.shape[1]
-
-    def product(weight):
-        return jnp.dot(
-            values[...],
-            weight[...].reshape(rows, weight.shape[-1]),
-            preferred_element_type=jnp.float32,
-        )
-
-    near[...] = product(near_weight)
-    of_far = product(far_weight)
-    far[...] = of_far
-    far_sent[...] = of_far.astype(jnp.bfloat16)
-
-
-def own_contribution(half, values, gathered, place, cols):
+    count = (len(refs) - 3) // 2
+    near, far, far_sent = refs[2 * count :]
+    for p in range(count):
+        place = slice(p * PIECE, (p + 1) * PIECE)
+        of_near, of_far = [
+            jnp.dot(values[...], weight[...].reshape(rows, PIECE), preferred_element_type=jnp.float32)
+            for weight in (refs[p], refs[count + p])
+        ]
+        near[:, place] = of_near
+        far[:, place] = of_far
+        far_sent[:, place] = of_far.astype(jnp.bfloat16)
+
+
+def own_contribution(half, values, pieces):
     tokens, kv = values.shape
-    rows_own = kv // (NX * NY)
-    result = pl.BlockSpec((tokens, cols), lambda i, h: (0, 0))
-    shape = (NY, NX, rows_own, cols)
+    shape = (NY, NX, kv // (NX * NY), PIECE)
+    width = len(pieces) * PIECE
+    result = pl.BlockSpec((tokens, width), lambda i, h: (0, 0))
+
+    def near(first, stride):
+        return pl.BlockSpec(shape, lambda i, h: (0, 0, first + h[0] * stride, 0))
+
+    def far(first, stride):
+        return pl.BlockSpec(shape, lambda i, h: (0, 0, first + (1 - h[0]) * stride, 0))
+
+    arrays = [array for array, _, _ in pieces]
     return pl.pallas_call(
         own_kernel,
         grid_spec=pltpu.PrefetchScalarGridSpec(
             num_scalar_prefetch=1,
             grid=(1,),
-            in_specs=[
-                pl.BlockSpec((tokens, kv), lambda i, h: (0, 0)),
-                pl.BlockSpec(shape, lambda i, h: (0, 0, h[0], place)),
-                pl.BlockSpec(shape, lambda i, h: (0, 0, 1 - h[0], place)),
-            ],
+            in_specs=[pl.BlockSpec((tokens, kv), lambda i, h: (0, 0))]
+            + [near(first, stride) for _, first, stride in pieces]
+            + [far(first, stride) for _, first, stride in pieces],
             out_specs=[result, result, result],
         ),
         out_shape=[
-            jax.ShapeDtypeStruct((tokens, cols), jnp.float32),
-            jax.ShapeDtypeStruct((tokens, cols), jnp.float32),
-            jax.ShapeDtypeStruct((tokens, cols), jnp.bfloat16),
+            jax.ShapeDtypeStruct((tokens, width), jnp.float32),
+            jax.ShapeDtypeStruct((tokens, width), jnp.float32),
+            jax.ShapeDtypeStruct((tokens, width), jnp.bfloat16),
         ],
         cost_estimate=pl.CostEstimate(
-            flops=4 * tokens * kv * cols, bytes_accessed=3 * 1024 * 1024, transcendentals=0
+            flops=4 * tokens * kv * width,
+            bytes_accessed=len(pieces) * 1536 * 1024,
+            transcendentals=0,
         ),
         compiler_params=PARAMS,
-    )(half.reshape(1).astype(jnp.int32), values, gathered, gathered)
+    )(half.reshape(1).astype(jnp.int32), values, *arrays, *arrays)
 
 
 def solve_kernel(y_ref, stats, block, sent, rows, left, right, matrix):
-    own = stats.shape[2]
-    size = block.shape[-1]
+    own, size = block.shape[2:]
     y = y_ref[0]
     for x in range(NX):
         for other in range(NY):
             place = slice((x * NY + other) * own, (x * NY + other + 1) * own)
             rows[place, :] = block[other, x]
-            left[place, :] = stats[other, x, :, :size].astype(jnp.float32)
-            right[place, :] = stats[other, x, :, size:].astype(jnp.float32)
+            for side, ref in enumerate((left, right)):
+                for piece in range(size // PIECE):
+                    group = side * (size // PIECE) + piece
+                    ref[place, piece * PIECE : (piece + 1) * PIECE] = stats[
+                        other, x, group * own : (group + 1) * own, :
+                    ].astype(jnp.float32)
     whole = rows[...]
     starts = [pl.multiple_of(x * NY * own + y * own, own) for x in range(NX)]
 
@@ -125,7 +196,7 @@
         grid=(1,),
         in_specs=[
             pl.BlockSpec(memory_space=pltpu.SMEM),
-            pl.BlockSpec((NY, NX, own, 2 * size), lambda i: (0, 0, 2, 0)),
+            pl.BlockSpec((NY, NX, 2 * own * size // PIECE, PIECE), lambda i: (0, 0, 0, 0)),
             pl.BlockSpec(block.shape, lambda i: (0, 0, 0, 0)),
         ],
         out_specs=pl.BlockSpec((NX, 5, own, size), lambda i: (0, 0, 0, 0)),
@@ -188,11 +259,11 @@
 
     value_full = lax.all_gather(value_grad[0], "tensor", axis=2, tiled=True)
 
-    stats = jnp.concatenate([left_stats[0], right_stats[0]], axis=2).astype(jnp.bfloat16)
-    halves = value_weight[0].reshape(rows_own, 2, width // 2).transpose(1, 0, 2)
-    halves = jnp.broadcast_to(halves.reshape(1, -1, width // 2), (NX, 2 * rows_own, width // 2))
-    first = exchange(jnp.concatenate([halves, stats], axis=1), X_GROUPS)
-    gathered = lax.all_gather(first, "dp", axis=0, axis_index_groups=Y_GROUPS)
+    per_half = width // (2 * PIECE)
+    early, late = 2 * SPLIT * rows_own, 2 * per_half * rows_own
+    first = exchange(pack(value_weight[0], left_stats[0], right_stats[0]), X_GROUPS)
+    first, value_full = lax.optimization_barrier((first, value_full))
+    gathered = lax.all_gather(first[:, :early], "dp", axis=0, axis_index_groups=Y_GROUPS)
 
     paired = jnp.take(value_full, order, axis=0).reshape(tokens, kv)
     inputs = stash[0].reshape(tokens, width)
@@ -208,54 +279,74 @@
         ]
     )
     over_x = exchange(partial, X_GROUPS)
-    over_x = jnp.sum(over_x.astype(jnp.float32), axis=0).astype(jnp.bfloat16)
-    by_y = over_x.reshape(NX, NY, rows_own, kv).transpose(1, 0, 2, 3)
-    over_y = exchange(by_y, Y_GROUPS)
+    last, _ = lax.optimization_barrier((first[:, early:late], partial))
+    last = lax.all_gather(last, "dp", axis=0, axis_index_groups=Y_GROUPS)
 
     value_own = value_full.reshape(tokens, NX, NY, rows_own).transpose(0, 2, 1, 3)
     value_own = value_own.reshape(tokens, kv)
     is_left = (section == 1) | (section == 2)
-    cols = width // 2 // CHUNKS
-    owns = [
-        own_contribution(jnp.where(is_left, 0, 1), value_own, gathered, k, cols)
-        for k in range(CHUNKS)
-    ]
-    over_y, _ = lax.optimization_barrier((over_y, owns))
-    own = jnp.sum(over_y.astype(jnp.float32), axis=0)
-    block = spread(own.astype(jnp.bfloat16), NY, Y_GROUPS)
-
+    half = jnp.where(is_left, 0, 1)
+    pieces = [(gathered, p, SPLIT) for p in range(SPLIT)] + [(last, 0, 1)]
+    owns = [own_contribution(half, value_own, part) for part in (pieces[:2], pieces[2:])]
+    to_mate = [(3, 2), (2, 3), (1, 0)]
+    mates = [lax.ppermute(owns[0][2], "section", to_mate)]
+
+    stats, _ = lax.optimization_barrier((first[:, late:], gathered))
+    stats = lax.all_gather(stats, "dp", axis=0, axis_index_groups=Y_GROUPS)
     top = top_grad.reshape(tokens, 2, width // 2)
     top_near = jnp.where(is_left, top[:, 0], top[:, 1])
     top_far = jnp.where(is_left, top[:, 1], top[:, 0])
+    over_x, _ = lax.optimization_barrier((over_x, (last, top_near, top_far, value_own)))
+    split_shape = jax.ShapeDtypeStruct((NY, NX, rows_own, kv), jnp.bfloat16)
+    by_y = whole_call(over_x_kernel, split_shape, over_x)
+    over_y = exchange(by_y, Y_GROUPS)
+
     f32, bf16 = jnp.float32, jnp.bfloat16
-    mates = [lax.ppermute(sent, "section", [(3, 2), (2, 3), (1, 0)]) for _, _, sent in owns]
-    helds, bases, seconds = [], [], []
-    for k, (near, _, _) in enumerate(owns):
-        mate = mates[k]
-        if k:
-            mate, _ = lax.optimization_barrier((mate, helds[-1]))
-        base = near + mate.astype(f32)
-        bases.append(base)
-        helds.append((top_near[:, k * cols : (k + 1) * cols].astype(f32) + base).astype(bf16))
-        seconds.append(lax.ppermute(helds[-1], "section", [(2, 1), (3, 0)]))
-    nears, fars = [], []
-    last = helds[-1]
-    for k, (near, far, _) in enumerate(owns):
-        part = slice(k * cols, (k + 1) * cols)
-        second, _ = lax.optimization_barrier((seconds[k], last))
-        updated = (second.astype(f32) + bases[k]).astype(bf16)
-        alone = (top_near[:, part].astype(f32) + near).astype(bf16)
-        passed = jnp.where(section == 0, second, jnp.where(section == 1, updated, helds[k]))
-        last = passed
-        nears.append(
-            jnp.where(section == 3, alone, jnp.where(section == 2, helds[k], updated))
-        )
-        third = lax.ppermute(passed, "section", [(1, 0), (0, 1), (3, 2)])
-        fars.append((third, far, top_far[:, part]))
-
-    block, _ = lax.optimization_barrier((block, helds))
-    sent = solve(y_index, gathered, block)
-    fars, _ = lax.optimization_barrier((fars, sent))
+    parts = [slice(0, 2 * PIECE), slice(2 * PIECE, 4 * PIECE)]
+
+    def hold(k, mate):
+        base = owns[k][0] + mate.astype(f32)
+        return base, (top_near[:, parts[k]].astype(f32) + base).astype(bf16)
+
+    def forward(k, second, base, held):
+        updated = (second.astype(f32) + base).astype(bf16)
+        alone = (top_near[:, parts[k]].astype(f32) + owns[k][0]).astype(bf16)
+        passed = jnp.where(section == 0, second, jnp.where(section == 1, updated, held))
+        near = jnp.where(section == 3, alone, jnp.where(section == 2, held, updated))
+        return passed, near
+
+    to_lower = [(2, 1), (3, 0)]
+    to_other = [(1, 0), (0, 1), (3, 2)]
+    over_y, _ = lax.optimization_barrier((over_y, owns))
+    own = whole_call(over_y_kernel, split_shape, over_y)
+    block = exchange(own, Y_GROUPS)
+
+    mate, _ = lax.optimization_barrier((mates[0], own))
+    base_0, held_0 = hold(0, mate)
+    second_0 = lax.ppermute(held_0, "section", to_lower)
+
+    far_1, _ = lax.optimization_barrier((owns[1][2], held_0))
+    mates.append(lax.ppermute(far_1, "section", to_mate))
+
+    second_0, _ = lax.optimization_barrier((second_0, own))
+    passed_0, near_0 = forward(0, second_0, base_0, held_0)
+    third_0 = lax.ppermute(passed_0, "section", to_other)
+
+    mate, _ = lax.optimization_barrier((mates[1], passed_0))
+    base_1, held_1 = hold(1, mate)
+    second_1 = lax.ppermute(held_1, "section", to_lower)
+
+    block, _ = lax.optimization_barrier((block, held_1))
+    sent = solve(y_index, stats, block)
+
+    second_1, _ = lax.optimization_barrier((second_1, sent))
+    passed_1, near_1 = forward(1, second_1, base_1, held_1)
+    third_1 = lax.ppermute(passed_1, "section", to_other)
+    nears = [near_0, near_1]
+    thirds, _ = lax.optimization_barrier(([third_0, third_1], passed_1))
+    fars = [
+        (third, owns[k][1], top_far[:, parts[k]]) for k, third in enumerate(thirds)
+    ]
     back = exchange(sent, X_GROUPS)
     weight_grad, new_left, new_right, roots = finish(
         refresh[0, 0], back, left_stats[0], right_stats[0]

time: 171 us -> 156 us (0.912)
  blocking collectives: 18.9 us -> 45.1 us
  waiting for transfers between devices: 53.6 us -> 27.4 us
  starting transfers between devices: 47.1 us -> 32.6 us
    all_gather x0 -> x1, blocking collectives: none -> 27.2 us  [per_device(): last = lax.all_gather(last, 'dp', axis=0, axis_index_groups=Y_GROUPS)]
    ppermute x6, waiting for transfers between devices: 29.2 us -> 11.1 us  [the longest x1 6.84 us: per_device(): mates.append(lax.ppermute(far_1, 'section', to_mate))]
    all_to_all x4, waiting for transfers between devices: 24.4 us -> 7.52 us  [exchange(): lax.all_to_all(block, 'dp', 0, 0, axis_index_groups=groups, tiled=True)]
    ppermute x6, starting transfers between devices: 25.1 us -> 9.63 us  [the longest x1 2.56 us: per_device(): third_1 = lax.ppermute(passed_1, 'section', to_other)]
    all_gather x1 -> x2, waiting for transfers between devices: 0.01 us -> 8.72 us  [the longest x1 8.72 us: per_device(): stats = lax.all_gather(stats, 'dp', axis=0, axis_index_groups=Y_GROUPS)]
    unnamed x38 -> x34, local copies, waits for them, and re-layouts: 3.45 us -> 6.72 us
    pallas_call x0 -> x3, Pallas kernels: none -> 2.72 us  [whole_call(): pl.pallas_call(kernel, in_specs=[vmem] * len(operands), out_specs=vmem, o...]
    reduce_sum x2 -> x0, other arithmetic: 2.36 us -> none  [the longest x1 1.24 us: per_device(): over_x = jnp.sum(over_x.astype(jnp.float32), axis=0).astype(jnp.bfloat16)]
  transfers between devices with their start and end apart: 11 -> 12, of which waited for: 3 -> 6; matrix products, arithmetic and copies ran while one was open for 13% -> 11% of each run, Pallas kernels for 3% -> 5%
where the time goes in v3:
time: 156 us; the launch traced here: 155 us
  blocking collectives  45.1 us (29%)
  starting transfers between devices  32.6 us (21%)
  waiting for transfers between devices  27.4 us (18%)
  between operations  14.4 us (9%)
  other arithmetic  13.3 us (9%)
  local copies, waits for them, and re-layouts  13 us (8%)
  Pallas kernels  7.99 us (5%)
    all_gather x1, blocking collectives, per_device(): last = lax.all_gather(last, 'dp', axis=0, axis_index_groups=Y_GROUPS)  27.2 us
    all_to_all x4, starting transfers between devices, exchange(): lax.all_to_all(block, 'dp', 0, 0, axis_index_groups=groups, tiled=True)  23 us
    all_to_all x1, blocking collectives, exchange(): lax.all_to_all(block, 'dp', 0, 0, axis_index_groups=groups, tiled=True)  11.1 us
    all_gather x1, waiting for transfers between devices, per_device(): stats = lax.all_gather(stats, 'dp', axis=0, axis_index_groups=Y_GROUPS)  8.72 us
    all_to_all x4, waiting for transfers between devices, exchange(): lax.all_to_all(block, 'dp', 0, 0, axis_index_groups=groups, tiled=True)  7.52 us
    all_gather x1, blocking collectives, per_device(): value_full = lax.all_gather(value_grad[0], 'tensor', axis=2, tiled=True)  6.84 us
    ppermute x1, waiting for transfers between devices, per_device(): mates.append(lax.ppermute(far_1, 'section', to_mate))  6.84 us
    unnamed x34, local copies, waits for them, and re-layouts  6.72 us
  transfers between devices with their start and end apart: 12, of which 6 were waited for; matrix products, arithmetic and copies ran while one was open for 11% of the time, Pallas kernels for 5%

profile of v3, /device:TPU:8, one launch (start us, length us, event | category | flops | bytes accessed | tf_op | source)
XLA Modules:
  0.0 155.1 jit_solution(11347361604261628509)
XLA Ops:
  7.2 0.9 copy-done.3
  8.1 0.9 copy-done.5
  9.0 0.8 copy-done.7
  9.8 0.8 shard_map.119
  10.6 4.3 %all-to-all-start = ((bf16[4,192,256]{2,1,0:T(8,128)(2,1)}), bf16[4,192,256]{2,1,0:T(8,128)(2,1)S(1)}, u32[]{:S(2)}, u32[]{:S(2)}) async-start(bf16[4,192,256]{2,1,0:T(8,128)(2,1)} %shard_map.119), calls=%async_computation | async-start | bytes 786432 | tf_op jit(solution)/shard_map/all_to_all | solution.py:20
  14.9 6.8 %all-gather = bf16[1,4,64,512]{3,2,1,0:T(8,128)(2,1)S(1)} all-gather(bf16[1,4,64,128]{3,2,1,0:T(8,128)(2,1)} %param.10), channel_id=2, replica_groups=mesh['section'=4,'dp'=32,'tensor'=4] {'tensor'}, dimensions={3}, use_global_device_ids=true | all-gather | bytes 327680 | tf_op jit(solution)/shard_map/all_gather | solution.py:260
  21.7 0.7 compare_and_fusion
  22.6 0.7 compare_select_fusion
  23.2 0.8 slice.46
  24.0 0.6 gather_fusion
  26.0 1.6 %pad_maximum_fusion = bf16[4,512,512]{2,1,0:T(8,128)(2,1)} fusion(bf16[1,512,512]{2,1,0:T(8,128)(2,1)S(1)} %fusion.3, bf16[1,512,512]{2,1,0:T(8,128)(2,1)S(1)} %fusion.2, bf16[1,512,512]{2,1,0:T(8,128)(2,1)S(1)} %fusion.1, bf16[1,512,512]{2,1,0:T(8,128)(2,1)S(1)} %fusion), kind=kLoop, calls=%fused_computation.1 | loop fusion | flops 3145728 | bytes 4194304 | tf_op jit(solution)/shard_map/stack | solution.py:270
  27.7 4.8 %all-to-all-start.1 = ((bf16[4,512,512]{2,1,0:T(8,128)(2,1)}), bf16[4,512,512]{2,1,0:T(8,128)(2,1)S(1)}, u32[]{:S(2)}, u32[]{:S(2)}) async-start(bf16[4,512,512]{2,1,0:T(8,128)(2,1)} %pad_maximum_fusion), calls=%async_computation.1 | async-start | bytes 4194304 | tf_op jit(solution)/shard_map/all_to_all | solution.py:20
  32.5 1.8 %reshape.150 = bf16[256,2,1024]{2,1,0:T(2,128)(2,1)S(1)} reshape(bf16[4,64,2048]{2,1,0:T(8,128)(2,1)} %param.8) | data formatting | bytes 2097152 | tf_op jit(solution)/shard_map/reshape | solution.py:296
  34.3 1.5 fusion.16
  35.8 1.3 select_bitcast_fusion
  37.8 27.2 %all-gather.2 = bf16[32,32,256]{2,1,0:T(8,128)(2,1)S(1)} all-gather(bf16[4,32,256]{2,1,0:T(8,128)(2,1)S(1)} %slice-done), channel_id=4, replica_groups={{0,4,8,12,16,20,24,28},{32,36,40,44,48,52,56,60},{64,68,72,76,80,84,88,..., dimensions={0}, use_global_device_ids=true | all-gather | bytes 589824 | tf_op jit(solution)/shard_map/all_gather | solution.py:283
  65.0 1.1 shard_map.121
  66.1 6.6 %all-to-all-start.2 = ((bf16[8,4,16,512]{3,2,1,0:T(8,128)(2,1)}), bf16[8,4,16,512]{3,2,1,0:T(8,128)(2,1)S(1)}, u32[]{:S(2)}, u32[]{:S(2)}) async-start(bf16[8,4,16,512]{3,2,1,0:T(8,128)(2,1)} %shard_map.121), calls=%async_computation.2 | async-start | bytes 1048576 | tf_op jit(solution)/shard_map/all_to_all | solution.py:20
  72.8 0.7 slice.53
  73.7 1.4 copy-done
  75.5 1.3 collective-permute-start
  76.8 0.4 shard_map.122
  77.3 0.8 copy-done.1
  78.1 6.5 %all-to-all-done.2.parts = bf16[8,4,16,512]{3,2,1,0:T(8,128)(2,1)S(1)} async-done(((bf16[8,4,16,512]{3,2,1,0:T(8,128)(2,1)}), bf16[8,4,16,512]{3,2,1,0:T(8,128)(2,1)S(1)}, u32[]{:S(2)}, u32[]{:S(2)}) %all-to-all-start.2) | async-done | bytes 524320 | tf_op jit(solution)/shard_map/all_to_all | solution.py:20
  84.6 0.9 shard_map.123
  85.5 3.2 %collective-permute-done = bf16[256,512]{1,0:T(8,128)(2,1)} collective-permute-done((bf16[256,512]{1,0:T(8,128)(2,1)S(1)}, bf16[256,512]{1,0:T(8,128)(2,1)}, u32[]{:S(2)}, u32[]{:S(2)}) %collective-permute-start) | collective-permute-done | bytes 262176 | tf_op jit(solution)/shard_map/ppermute | solution.py:292
  88.6 1.1 fusion.5
  89.8 1.3 collective-permute-start.1
  91.1 7.2 %all-to-all-start.3 = ((bf16[8,4,16,512]{3,2,1,0:T(8,128)(2,1)}), bf16[8,4,16,512]{3,2,1,0:T(8,128)(2,1)S(1)}, u32[]{:S(2)}, u32[]{:S(2)}) async-start(bf16[8,4,16,512]{3,2,1,0:T(8,128)(2,1)} %shard_map.123), calls=%async_computation.3 | async-start | bytes 1048576 | tf_op jit(solution)/shard_map/all_to_all | solution.py:20
  98.3 1.3 collective-permute-start.2
  99.6 1.1 collective-permute-done.1
  100.7 1.2 fusion.11
  101.9 1.7 %select_select_fusion.1 = bf16[256,512]{1,0:T(8,128)(2,1)} fusion(bf16[256,512]{1,0:T(8,128)(2,1)} %collective-permute-done.1, bf16[256,512]{1,0:T(8,128)(2,1)S(1)} %get-tuple-element.54, bf16[256,512]{1,0:T(8,128)(2,1)S(1)} %fusion.5, pred[]{:T(512)S(6)} %eq.10, pred[]{:T(512)S(6)} %eq.13), kind=kLoop, calls=%fused_computation.43 | loop fusion | flops 262144 | bytes 1048578 | tf_op jit(solution)/shard_map/jit(_where)/select_n | solution.py:314
  103.6 6.8 %collective-permute-done.2 = bf16[256,512]{1,0:T(8,128)(2,1)S(1)} collective-permute-done((bf16[256,512]{1,0:T(8,128)(2,1)S(1)}, bf16[256,512]{1,0:T(8,128)(2,1)S(1)}, u32[]{:S(2)}, u32[]{:S(2)}) %collective-permute-start.2) | collective-permute-done | bytes 262176 | tf_op jit(solution)/shard_map/ppermute | solution.py:329
  110.5 0.6 copy-done.15
  111.1 1.3 collective-permute-start.3
  112.4 1.9 %collective-permute-start.4 = (bf16[256,512]{1,0:T(8,128)(2,1)}, bf16[256,512]{1,0:T(8,128)(2,1)}, u32[]{:S(2)}, u32[]{:S(2)}) collective-permute-start(bf16[256,512]{1,0:T(8,128)(2,1)} %select_select_fusion.1), channel_id=1, source_target_pairs={{128,0},{0,128},{384,256},{129,1},{1,129},{385,257},{130,2},{2,130... | collective-permute-start | bytes 786440 | tf_op jit(solution)/shard_map/ppermute | solution.py:333
  114.4 1.0 all-to-all-done.3.block
  115.4 8.7 %all-gather.9.cloned.1.call-done = bf16[32,64,256]{2,1,0:T(8,128)(2,1)} async-done(((bf16[4,64,256]{2,1,0:T(8,128)(2,1)}), bf16[32,64,256]{2,1,0:T(8,128)(2,1)}) %all-gather.9.cloned.1.call-update) | async-done | bytes 1048592 | tf_op jit(solution)/shard_map/all_gather | solution.py:295
  124.1 1.2 copy-done.9
  125.3 3.0 %shard_map.124 = bf16[4,5,16,512]{3,2,1,0:T(8,128)(2,1)S(1)} custom-call(s32[1]{0:T(128)} %bitcast.18.y_ref, bf16[8,4,64,256]{3,2,1,0:T(8,128)(2,1)S(1)} %bitcast.55, bf16[8,4,16,512]{3,2,1,0:T(8,128)(2,1)S(1)} %all-to-all-done.3.block), custom_call_target="tpu_custom_call" | custom-call | flops 805306368 | bytes 2097152 | tf_op jit(solution)/shard_map/pallas_call | solution.py:194
  128.4 1.3 fusion.10
  129.8 1.0 select_select_fusion
  130.8 2.6 %collective-permute-start.5 = (bf16[256,512]{1,0:T(8,128)(2,1)S(1)}, bf16[256,512]{1,0:T(8,128)(2,1)S(1)}, u32[]{:S(2)}, u32[]{:S(2)}) collective-permute-start(bf16[256,512]{1,0:T(8,128)(2,1)S(1)} %select_select_fusion), channel_id=1, source_target_pairs={{128,0},{0,128},{384,256},{129,1},{1,129},{385,257},{130,2},{2,130... | collective-permute-start | bytes 786440 | tf_op jit(solution)/shard_map/ppermute | solution.py:344
  133.3 11.1 %all_to_all.25.back = bf16[4,5,16,512]{3,2,1,0:T(8,128)(2,1)S(1)} all-to-all(bf16[4,5,16,512]{3,2,1,0:T(8,128)(2,1)S(1)} %shard_map.124), channel_id=1, replica_groups={{0,32,64,96},{4,36,68,100},{8,40,72,104},{12,44,76,108},{16,48,80,112},..., dimensions={0} | all-to-all | bytes 655360 | tf_op jit(solution)/shard_map/all_to_all | solution.py:20
  144.4 1.4 shard_map.125
  145.8 1.2 fusion.8
  147.2 1.1 pad_maximum_fusion.1
  (54 shorter events, 3.3 us)
Async XLA Ops:
  7.2 0.9 copy-start.3
  8.1 0.9 copy-start.5
  9.0 0.8 copy-start.7
  9.8 14.9 %copy-start.14 = (bf16[1,4,64,2048]{3,2,1,0:T(8,128)(2,1)S(1)}, bf16[1,4,64,2048]{3,2,1,0:T(8,128)(2,1)}, u32[]{:S(2)}) copy-start(bf16[1,4,64,2048]{3,2,1,0:T(8,128)(2,1)} %param.9) | copy-start | bytes 3145732
  10.6 12.6 %all-to-all-start = ((bf16[4,192,256]{2,1,0:T(8,128)(2,1)}), bf16[4,192,256]{2,1,0:T(8,128)(2,1)S(1)}, u32[]{:S(2)}, u32[]{:S(2)}) async-start(bf16[4,192,256]{2,1,0:T(8,128)(2,1)} %shard_map.119), calls=%async_computation | async-start | bytes 786432 | tf_op jit(solution)/shard_map/all_to_all | solution.py:20
  14.9 58.5 %all-gather.7.cloned.1.call-start = ((), (), s32[]{:S(2)}) async-start(), calls=%async_computation.5 | async-start | bytes 1769472 | tf_op jit(solution)/shard_map/all_gather | solution.py:266
  23.2 4.4 %copy-start.12 = (bf16[4,192,256]{2,1,0:T(8,128)(2,1)}, bf16[4,192,256]{2,1,0:T(8,128)(2,1)S(1)}, u32[]{:S(2)}) copy-start(bf16[4,192,256]{2,1,0:T(8,128)(2,1)S(1)} %all-to-all-done) | copy-start | bytes 1179652
  27.7 37.4 %all-to-all-start.1 = ((bf16[4,512,512]{2,1,0:T(8,128)(2,1)}), bf16[4,512,512]{2,1,0:T(8,128)(2,1)S(1)}, u32[]{:S(2)}, u32[]{:S(2)}) async-start(bf16[4,512,512]{2,1,0:T(8,128)(2,1)} %pad_maximum_fusion), calls=%async_computation.1 | async-start | bytes 4194304 | tf_op jit(solution)/shard_map/all_to_all | solution.py:20
  35.8 2.0 %slice-start = ((bf16[4,192,256]{2,1,0:T(8,128)(2,1)}), bf16[4,32,256]{2,1,0:T(8,128)(2,1)S(1)}, s32[]{:S(2)}) async-start(bf16[4,192,256]{2,1,0:T(8,128)(2,1)} %copy-done.12), calls=%async_computation.7 | async-start | bytes 131072 | tf_op jit(solution)/shard_map/slice | solution.py:282
  37.8 35.0 %copy-start.13 = (bf16[4,192,256]{2,1,0:T(8,128)(2,1)S(1)}, bf16[4,192,256]{2,1,0:T(8,128)(2,1)}, u32[]{:S(2)}) copy-start(bf16[4,192,256]{2,1,0:T(8,128)(2,1)} %copy-done.12) | copy-start | bytes 1179652
  66.1 18.5 %all-to-all-start.2 = ((bf16[8,4,16,512]{3,2,1,0:T(8,128)(2,1)}), bf16[8,4,16,512]{3,2,1,0:T(8,128)(2,1)S(1)}, u32[]{:S(2)}, u32[]{:S(2)}) async-start(bf16[8,4,16,512]{3,2,1,0:T(8,128)(2,1)} %shard_map.121), calls=%async_computation.2 | async-start | bytes 1048576 | tf_op jit(solution)/shard_map/all_to_all | solution.py:20
  72.8 51.3 %all-gather.9.cloned.1.call-start = ((), (), s32[]{:S(2)}) async-start(), calls=%async_computation.6 | async-start | bytes 1179648 | tf_op jit(solution)/shard_map/all_gather | solution.py:295
  73.6 1.4 copy-start
  75.5 13.1 %collective-permute-start = (bf16[256,512]{1,0:T(8,128)(2,1)S(1)}, bf16[256,512]{1,0:T(8,128)(2,1)}, u32[]{:S(2)}, u32[]{:S(2)}) collective-permute-start(bf16[256,512]{1,0:T(8,128)(2,1)S(1)} %get-tuple-element.32), channel_id=1, source_target_pairs={{384,256},{256,384},{128,0},{385,257},{257,385},{129,1},{386,258},... | collective-permute-start | bytes 786440 | tf_op jit(solution)/shard_map/ppermute | solution.py:292
  77.3 0.8 copy-start.1
  78.1 22.6 %copy-start.10 = (bf16[256,1024]{1,0:T(8,128)(2,1)S(1)}, bf16[256,1024]{1,0:T(8,128)(2,1)}, u32[]{:S(2)}) copy-start(bf16[256,1024]{1,0:T(8,128)(2,1)} %get-tuple-element.58) | copy-start | bytes 1572868
  89.8 10.9 %collective-permute-start.1 = (bf16[256,512]{1,0:T(8,128)(2,1)S(1)}, bf16[256,512]{1,0:T(8,128)(2,1)}, u32[]{:S(2)}, u32[]{:S(2)}) collective-permute-start(bf16[256,512]{1,0:T(8,128)(2,1)S(1)} %fusion.5), channel_id=1, source_target_pairs={{256,128},{384,0},{257,129},{385,1},{258,130},{386,2},{259,131},{3... | collective-permute-start | bytes 786440 | tf_op jit(solution)/shard_map/ppermute | solution.py:326
  91.1 24.3 %all-to-all-start.3 = ((bf16[8,4,16,512]{3,2,1,0:T(8,128)(2,1)}), bf16[8,4,16,512]{3,2,1,0:T(8,128)(2,1)S(1)}, u32[]{:S(2)}, u32[]{:S(2)}) async-start(bf16[8,4,16,512]{3,2,1,0:T(8,128)(2,1)} %shard_map.123), calls=%async_computation.3 | async-start | bytes 1048576 | tf_op jit(solution)/shard_map/all_to_all | solution.py:20
  98.3 12.1 %collective-permute-start.2 = (bf16[256,512]{1,0:T(8,128)(2,1)S(1)}, bf16[256,512]{1,0:T(8,128)(2,1)S(1)}, u32[]{:S(2)}, u32[]{:S(2)}) collective-permute-start(bf16[256,512]{1,0:T(8,128)(2,1)S(1)} %get-tuple-element.42), channel_id=1, source_target_pairs={{384,256},{256,384},{128,0},{385,257},{257,385},{129,1},{386,258},... | collective-permute-start | bytes 786440 | tf_op jit(solution)/shard_map/ppermute | solution.py:329
  110.4 0.7 copy-start.15
  111.1 17.3 %collective-permute-start.3 = (bf16[256,512]{1,0:T(8,128)(2,1)S(1)}, bf16[256,512]{1,0:T(8,128)(2,1)}, u32[]{:S(2)}, u32[]{:S(2)}) collective-permute-start(bf16[256,512]{1,0:T(8,128)(2,1)S(1)} %fusion.7), channel_id=1, source_target_pairs={{256,128},{384,0},{257,129},{385,1},{258,130},{386,2},{259,131},{3... | collective-permute-start | bytes 786440 | tf_op jit(solution)/shard_map/ppermute | solution.py:337
  112.4 33.3 %collective-permute-start.4 = (bf16[256,512]{1,0:T(8,128)(2,1)}, bf16[256,512]{1,0:T(8,128)(2,1)}, u32[]{:S(2)}, u32[]{:S(2)}) collective-permute-start(bf16[256,512]{1,0:T(8,128)(2,1)} %select_select_fusion.1), channel_id=1, source_target_pairs={{128,0},{0,128},{384,256},{129,1},{1,129},{385,257},{130,2},{2,130... | collective-permute-start | bytes 786440 | tf_op jit(solution)/shard_map/ppermute | solution.py:333
  124.1 1.2 copy-start.9
  125.3 3.1 %copy-start.16 = (bf16[256,512]{1,0:T(8,128)(2,1)S(1)}, bf16[256,512]{1,0:T(8,128)(2,1)}, u32[]{:S(2)}) copy-start(bf16[256,512]{1,0:T(8,128)(2,1)} %copy-done.15) | copy-start | bytes 786436
  128.4 16.0 %copy-start.4 = (f32[1,4,16,512]{3,2,1,0:T(8,128)S(1)}, f32[1,4,16,512]{3,2,1,0:T(8,128)}, u32[]{:S(2)}) copy-start(f32[1,4,16,512]{3,2,1,0:T(8,128)} %param.12) | copy-start | bytes 393220
  128.4 16.0 %copy-start.6 = (f32[1,4,16,512]{3,2,1,0:T(8,128)S(1)}, f32[1,4,16,512]{3,2,1,0:T(8,128)}, u32[]{:S(2)}) copy-start(f32[1,4,16,512]{3,2,1,0:T(8,128)} %param.13) | copy-start | bytes 393220
  128.4 16.0 %copy-start.8 = (s32[1,1,2]{2,1,0:T(1,128)S(1)}, s32[1,1,2]{2,1,0:T(1,128)}, u32[]{:S(2)}) copy-start(s32[1,1,2]{2,1,0:T(1,128)} %param.14) | copy-start | bytes 28
  128.4 17.4 %copy-start.2 = (f32[256,512]{1,0:T(8,128)S(1)}, f32[256,512]{1,0:T(8,128)}, u32[]{:S(2)}) copy-start(f32[256,512]{1,0:T(8,128)} %copy-done.1) | copy-start | bytes 1572868
  128.4 17.4 %copy-start.11 = (bf16[256,1024]{1,0:T(8,128)(2,1)S(1)}, bf16[256,1024]{1,0:T(8,128)(2,1)}, u32[]{:S(2)}) copy-start(bf16[256,1024]{1,0:T(8,128)(2,1)} %get-tuple-element.57) | copy-start | bytes 1572868
  130.8 15.0 %collective-permute-start.5 = (bf16[256,512]{1,0:T(8,128)(2,1)S(1)}, bf16[256,512]{1,0:T(8,128)(2,1)S(1)}, u32[]{:S(2)}, u32[]{:S(2)}) collective-permute-start(bf16[256,512]{1,0:T(8,128)(2,1)S(1)} %select_select_fusion), channel_id=1, source_target_pairs={{128,0},{0,128},{384,256},{129,1},{1,129},{385,257},{130,2},{2,130... | collective-permute-start | bytes 786440 | tf_op jit(solution)/shard_map/ppermute | solution.py:344
Sparse Core Ops, SparseCore 0:
  24.1 47.2 all-gather.6
  76.2 47.8 all-gather.8

commit v4 on v3

--- a/solution.py
+++ b/solution.py
@@ -1,3 +1,5 @@
+import functools
+
 import jax
 import jax.numpy as jnp
 from jax import lax
@@ -14,6 +16,7 @@
 PIECE = 256
 SPLIT = 3
 PARAMS = pltpu.CompilerParams(vmem_limit_bytes=40 * 1024 * 1024)
+WIDE = pltpu.CompilerParams(vmem_limit_bytes=56 * 1024 * 1024)
 
 
 def exchange(block, groups):
@@ -28,26 +31,74 @@
     def put(x, group, piece):
         packed[x, group * own : (group + 1) * own, :] = piece
 
-    for h in range(2):
-        for p in range(per_half):
-            group = h * SPLIT + p if p < SPLIT else 2 * SPLIT + h * rest + p - SPLIT
-            column = (h * per_half + p) * PIECE
-            for x in range(NX):
-                put(x, group, weight[:, column : column + PIECE])
-    group = 2 * per_half
+    group = 0
     for ref in (left, right):
         for p in range(ref.shape[2] // PIECE):
             for x in range(NX):
                 put(x, group, ref[x, :, p * PIECE : (p + 1) * PIECE].astype(jnp.bfloat16))
             group += 1
+    for h in range(2):
+        for p in range(per_half):
+            place = h * SPLIT + p if p < SPLIT else 2 * SPLIT + h * rest + p - SPLIT
+            column = (h * per_half + p) * PIECE
+            for x in range(NX):
+                put(x, group + place, weight[:, column : column + PIECE])
 
 
 def pack(weight, left, right):
     own, width = weight.shape
     rows = own * (width + 2 * left.shape[2]) // PIECE
-    return whole_call(
-        pack_kernel, jax.ShapeDtypeStruct((NX, rows, PIECE), jnp.bfloat16), weight, left, right
-    )
+    return pl.pallas_call(
+        pack_kernel,
+        grid=(1,),
+        in_specs=[
+            pl.BlockSpec(weight.shape, lambda i: (0, 0)),
+            pl.BlockSpec(left.shape, lambda i: (0, 0, 0)),
+            pl.BlockSpec(right.shape, lambda i: (0, 0, 0)),
+        ],
+        out_specs=pl.BlockSpec((NX, rows, PIECE), lambda i: (0, 0, 0)),
+        out_shape=jax.ShapeDtypeStruct((NX, rows, PIECE), jnp.bfloat16),
+        cost_estimate=pl.CostEstimate(
+            flops=1024, bytes_accessed=1024 * 1024, transcendentals=0
+        ),
+        compiler_params=WIDE,
+    )(weight, left, right)
+
+
+def partial_kernel(order, values, inputs, result):
+    total = 0.0
+    for k in range(inputs.shape[0]):
+        total += lax.dot_general(
+            values[order[k]],
+            inputs[k],
+            (((0,), (0,)), ((), ())),
+            preferred_element_type=jnp.float32,
+        )
+    result[0] = total.astype(jnp.bfloat16)
+
+
+def partial_gradient(order, values, inputs):
+    micro, tokens, kv = values.shape
+    blocks = inputs.shape[2] // kv
+    return pl.pallas_call(
+        partial_kernel,
+        grid_spec=pltpu.PrefetchScalarGridSpec(
+            num_scalar_prefetch=1,
+            grid=(blocks,),
+            in_specs=[
+                pl.BlockSpec((micro, tokens, kv), lambda b, o: (0, 0, 0)),
+                pl.BlockSpec((micro, tokens, kv), lambda b, o: (0, 0, b)),
+            ],
+            out_specs=pl.BlockSpec((1, kv, kv), lambda b, o: (b, 0, 0)),
+        ),
+        out_shape=jax.ShapeDtypeStruct((blocks, kv, kv), jnp.bfloat16),
+        cost_estimate=pl.CostEstimate(
+            flops=2 * micro * tokens * kv * kv * blocks,
+            bytes_accessed=3 * 1024 * 1024,
+            transcendentals=0,
+        ),
+        compiler_params=PARAMS,
+    )(order, values, inputs)
 
 
 def over_x_kernel(parts, result):
@@ -136,19 +187,16 @@
     )(half.reshape(1).astype(jnp.int32), values, *arrays, *arrays)
 
 
-def solve_kernel(y_ref, stats, block, sent, rows, left, right, matrix):
+def solve_kernel(y_ref, left_0, left_1, right_0, right_1, block, sent, rows, left, right, matrix):
     own, size = block.shape[2:]
     y = y_ref[0]
     for x in range(NX):
         for other in range(NY):
             place = slice((x * NY + other) * own, (x * NY + other + 1) * own)
             rows[place, :] = block[other, x]
-            for side, ref in enumerate((left, right)):
-                for piece in range(size // PIECE):
-                    group = side * (size // PIECE) + piece
-                    ref[place, piece * PIECE : (piece + 1) * PIECE] = stats[
-                        other, x, group * own : (group + 1) * own, :
-                    ].astype(jnp.float32)
+            for ref, pieces in ((left, (left_0, left_1)), (right, (right_0, right_1))):
+                for p, piece in enumerate(pieces):
+                    ref[place, p * PIECE : (p + 1) * PIECE] = piece[other, x].astype(jnp.float32)
     whole = rows[...]
     starts = [pl.multiple_of(x * NY * own + y * own, own) for x in range(NX)]
 
@@ -189,6 +237,10 @@
             sent[x, 3 + side] = root[part]
 
 
+def group_place(group, i):
+    return 0, 0, group, 0
+
+
 def solve(y_index, gathered, block):
     own, size = block.shape[2:]
     return pl.pallas_call(
@@ -196,7 +248,10 @@
         grid=(1,),
         in_specs=[
             pl.BlockSpec(memory_space=pltpu.SMEM),
-            pl.BlockSpec((NY, NX, 2 * own * size // PIECE, PIECE), lambda i: (0, 0, 0, 0)),
+            *[
+                pl.BlockSpec((NY, NX, own, PIECE), functools.partial(group_place, g))
+                for g in range(4)
+            ],
             pl.BlockSpec(block.shape, lambda i: (0, 0, 0, 0)),
         ],
         out_specs=pl.BlockSpec((NX, 5, own, size), lambda i: (0, 0, 0, 0)),
@@ -211,7 +266,7 @@
             flops=3 * 2 * size**3, bytes_accessed=2 * 1024 * 1024, transcendentals=0
         ),
         compiler_params=PARAMS,
-    )(y_index.reshape(1).astype(jnp.int32), gathered, block)
+    )(y_index.reshape(1).astype(jnp.int32), *[gathered] * 4, block)
 
 
 def finish_kernel(refresh, back, left_stats, right_stats, weight_grad, new_left, new_right, roots):
@@ -251,7 +306,6 @@
 def per_device(top_grad, stash, value_grad, value_weight, left_stats, right_stats, refresh, order):
     micro, tok_dev, width = top_grad.shape
     rows_own = value_weight.shape[1]
-    blocks = left_stats.shape[1]
     kv = left_stats.shape[3]
     tokens = micro * tok_dev
     section = lax.axis_index("section")
@@ -260,26 +314,18 @@
     value_full = lax.all_gather(value_grad[0], "tensor", axis=2, tiled=True)
 
     per_half = width // (2 * PIECE)
-    early, late = 2 * SPLIT * rows_own, 2 * per_half * rows_own
+    groups = 2 * kv // PIECE
+    early = (groups + 2 * SPLIT) * rows_own
     first = exchange(pack(value_weight[0], left_stats[0], right_stats[0]), X_GROUPS)
     first, value_full = lax.optimization_barrier((first, value_full))
-    gathered = lax.all_gather(first[:, :early], "dp", axis=0, axis_index_groups=Y_GROUPS)
-
-    paired = jnp.take(value_full, order, axis=0).reshape(tokens, kv)
-    inputs = stash[0].reshape(tokens, width)
-    partial = jnp.stack(
-        [
-            lax.dot_general(
-                paired,
-                inputs[:, b * kv : (b + 1) * kv],
-                (((0,), (0,)), ((), ())),
-                preferred_element_type=jnp.float32,
-            ).astype(jnp.bfloat16)
-            for b in range(blocks)
-        ]
-    )
+    late = groups * rows_own
+    gathered = lax.all_gather(first[:, late:early], "dp", axis=0, axis_index_groups=Y_GROUPS)
+    stats, _ = lax.optimization_barrier((first[:, :late], gathered))
+    stats = lax.all_gather(stats, "dp", axis=0, axis_index_groups=Y_GROUPS)
+
+    partial = partial_gradient(order, value_full, stash[0])
     over_x = exchange(partial, X_GROUPS)
-    last, _ = lax.optimization_barrier((first[:, early:late], partial))
+    last, _ = lax.optimization_barrier((first[:, early:], partial))
     last = lax.all_gather(last, "dp", axis=0, axis_index_groups=Y_GROUPS)
 
     value_own = value_full.reshape(tokens, NX, NY, rows_own).transpose(0, 2, 1, 3)
@@ -291,29 +337,36 @@
     to_mate = [(3, 2), (2, 3), (1, 0)]
     mates = [lax.ppermute(owns[0][2], "section", to_mate)]
 
-    stats, _ = lax.optimization_barrier((first[:, late:], gathered))
-    stats = lax.all_gather(stats, "dp", axis=0, axis_index_groups=Y_GROUPS)
-    top = top_grad.reshape(tokens, 2, width // 2)
-    top_near = jnp.where(is_left, top[:, 0], top[:, 1])
-    top_far = jnp.where(is_left, top[:, 1], top[:, 0])
+    top = top_grad.reshape(tokens, width)
+    cols = 2 * PIECE
+    left_top, right_top = [
+        [top[:, start + k * cols : start + (k + 1) * cols] for k in range(2)]
+        for start in (0, width // 2)
+    ]
+    top_near = [jnp.where(is_left, a, b) for a, b in zip(left_top, right_top)]
+    top_far = [jnp.where(is_left, b, a) for a, b in zip(left_top, right_top)]
     over_x, _ = lax.optimization_barrier((over_x, (last, top_near, top_far, value_own)))
     split_shape = jax.ShapeDtypeStruct((NY, NX, rows_own, kv), jnp.bfloat16)
     by_y = whole_call(over_x_kernel, split_shape, over_x)
     over_y = exchange(by_y, Y_GROUPS)
 
     f32, bf16 = jnp.float32, jnp.bfloat16
-    parts = [slice(0, 2 * PIECE), slice(2 * PIECE, 4 * PIECE)]
 
     def hold(k, mate):
-        base = owns[k][0] + mate.astype(f32)
-        return base, (top_near[:, parts[k]].astype(f32) + base).astype(bf16)
-
-    def forward(k, second, base, held):
-        updated = (second.astype(f32) + base).astype(bf16)
-        alone = (top_near[:, parts[k]].astype(f32) + owns[k][0]).astype(bf16)
-        passed = jnp.where(section == 0, second, jnp.where(section == 1, updated, held))
-        near = jnp.where(section == 3, alone, jnp.where(section == 2, held, updated))
-        return passed, near
+        return (top_near[k].astype(f32) + (owns[k][0] + mate.astype(f32))).astype(bf16)
+
+    def update(second, near, mate):
+        return (second.astype(f32) + (near + mate.astype(f32))).astype(bf16)
+
+    def forward(k, second, mate, held):
+        updated = update(second, owns[k][0], mate)
+        return jnp.where(section == 0, second, jnp.where(section == 1, updated, held))
+
+    def finished(k, second, mate, held, after):
+        second, mate, near, _ = lax.optimization_barrier((second, mate, owns[k][0], after))
+        alone = (top_near[k].astype(f32) + near).astype(bf16)
+        updated = update(second, near, mate)
+        return jnp.where(section == 3, alone, jnp.where(section == 2, held, updated))
 
     to_lower = [(2, 1), (3, 0)]
     to_other = [(1, 0), (0, 1), (3, 2)]
@@ -321,32 +374,33 @@
     own = whole_call(over_y_kernel, split_shape, over_y)
     block = exchange(own, Y_GROUPS)
 
-    mate, _ = lax.optimization_barrier((mates[0], own))
-    base_0, held_0 = hold(0, mate)
+    mate_0, _ = lax.optimization_barrier((mates[0], own))
+    held_0 = hold(0, mate_0)
     second_0 = lax.ppermute(held_0, "section", to_lower)
 
     far_1, _ = lax.optimization_barrier((owns[1][2], held_0))
     mates.append(lax.ppermute(far_1, "section", to_mate))
 
     second_0, _ = lax.optimization_barrier((second_0, own))
-    passed_0, near_0 = forward(0, second_0, base_0, held_0)
+    passed_0 = forward(0, second_0, mate_0, held_0)
     third_0 = lax.ppermute(passed_0, "section", to_other)
 
-    mate, _ = lax.optimization_barrier((mates[1], passed_0))
-    base_1, held_1 = hold(1, mate)
+    mate_1, _ = lax.optimization_barrier((mates[1], passed_0))
+    held_1 = hold(1, mate_1)
     second_1 = lax.ppermute(held_1, "section", to_lower)
 
     block, _ = lax.optimization_barrier((block, held_1))
     sent = solve(y_index, stats, block)
 
     second_1, _ = lax.optimization_barrier((second_1, sent))
-    passed_1, near_1 = forward(1, second_1, base_1, held_1)
+    passed_1 = forward(1, second_1, mate_1, held_1)
     third_1 = lax.ppermute(passed_1, "section", to_other)
-    nears = [near_0, near_1]
-    thirds, _ = lax.optimization_barrier(([third_0, third_1], passed_1))
-    fars = [
-        (third, owns[k][1], top_far[:, parts[k]]) for k, third in enumerate(thirds)
+    nears = [
+        finished(0, second_0, mate_0, held_0, passed_1),
+        finished(1, second_1, mate_1, held_1, passed_1),
     ]
+    thirds, _ = lax.optimization_barrier(([third_0, third_1], nears))
+    fars = [(third, owns[k][1], top_far[k]) for k, third in enumerate(thirds)]
     back = exchange(sent, X_GROUPS)
     weight_grad, new_left, new_right, roots = finish(
         refresh[0, 0], back, left_stats[0], right_stats[0]

time: 156 us -> 155 us (level)
  blocking collectives: 45.1 us -> 34 us
  waiting for transfers between devices: 27.4 us -> 35.2 us
  local copies, waits for them, and re-layouts: 13 us -> 7.16 us
  Pallas kernels: 7.99 us -> 13.5 us
  starting transfers between devices: 32.6 us -> 36 us
    all_to_all x1 -> x0, blocking collectives: 11.1 us -> none  [exchange(): lax.all_to_all(block, 'dp', 0, 0, axis_index_groups=groups, tiled=True)]
    all_to_all x4 -> x5, waiting for transfers between devices: 7.52 us -> 16.5 us  [exchange(): lax.all_to_all(block, 'dp', 0, 0, axis_index_groups=groups, tiled=True)]
    pallas_call x0 -> x2, Pallas kernels: none -> 5.5 us  [the longest x1 3.64 us: partial_gradient(): pl.pallas_call(partial_kernel, grid_spec=pltpu.PrefetchScalarGridSpec(num...]
    all_to_all x4 -> x5, starting transfers between devices: 23 us -> 25.4 us  [exchange(): lax.all_to_all(block, 'dp', 0, 0, axis_index_groups=groups, tiled=True)]
    unnamed x34 -> x38, local copies, waits for them, and re-layouts: 6.72 us -> 4.8 us
    all_gather x1, waiting for transfers between devices: 8.72 us -> 6.88 us  [per_device(): stats = lax.all_gather(stats, 'dp', axis=0, axis_index_groups=Y_GROUPS)]
    reshape x1 -> x0, local copies, waits for them, and re-layouts: 1.83 us -> none  [per_device(): top = top_grad.reshape(tokens, 2, width // 2)]
    another operation x1 -> x0, other arithmetic: 1.6 us -> none  [per_device(): jnp.stack([lax.dot_general(paired, inputs[:, b * kv:(b + 1) * kv], (((0,)...]
  transfers between devices with their start and end apart: 12 -> 13, of which waited for: 6 -> 8; matrix products, arithmetic and copies ran while one was open for 11% -> 8% of each run, Pallas kernels for 5% -> 8%
where the time goes in v4:
time: 155 us; the launch traced here: 154 us
  starting transfers between devices  36 us (23%)
  waiting for transfers between devices  35.2 us (23%)
  blocking collectives  34 us (22%)
  between operations  14.3 us (9%)
  other arithmetic  14.2 us (9%)
  Pallas kernels  13.5 us (9%)
  local copies, waits for them, and re-layouts  7.16 us (5%)
    all_gather x1, blocking collectives, per_device(): last = lax.all_gather(last, 'dp', axis=0, axis_index_groups=Y_GROUPS)  27.2 us
    all_to_all x5, starting transfers between devices, exchange(): lax.all_to_all(block, 'dp', 0, 0, axis_index_groups=groups, tiled=True)  25.4 us
    all_to_all x5, waiting for transfers between devices, exchange(): lax.all_to_all(block, 'dp', 0, 0, axis_index_groups=groups, tiled=True)  16.5 us
    ppermute x1, waiting for transfers between devices, per_device(): mates.append(lax.ppermute(far_1, 'section', to_mate))  8.11 us
    all_gather x1, waiting for transfers between devices, per_device(): stats = lax.all_gather(stats, 'dp', axis=0, axis_index_groups=Y_GROUPS)  6.88 us
    all_gather x1, blocking collectives, per_device(): value_full = lax.all_gather(value_grad[0], 'tensor', axis=2, tiled=True)  6.84 us
    unnamed x38, local copies, waits for them, and re-layouts  4.8 us
    select_n x2, other arithmetic, forward(): jnp.where(section == 0, second, jnp.where(section == 1, updated, held))  3.95 us
  transfers between devices with their start and end apart: 13, of which 8 were waited for; matrix products, arithmetic and copies ran while one was open for 8% of the time, Pallas kernels for 8%

profile of v4, /device:TPU:8, one launch (start us, length us, event | category | flops | bytes accessed | tf_op | source)
XLA Modules:
  0.0 154.4 jit_solution(4436623140835023799)
XLA Ops:
  7.2 1.9 %shard_map.119 = bf16[4,192,256]{2,1,0:T(8,128)(2,1)} custom-call(bf16[16,2048]{1,0:T(8,128)(2,1)} %bitcast.51, f32[4,16,512]{2,1,0:T(8,128)} %bitcast.39, f32[4,16,512]{2,1,0:T(8,128)} %bitcast.41), custom_call_target="tpu_custom_call" | custom-call | flops 1024 | bytes 1048576 | tf_op jit(solution)/shard_map/pallas_call | solution.py:51
  9.0 4.3 %all-to-all-start = ((bf16[4,192,256]{2,1,0:T(8,128)(2,1)}), bf16[4,192,256]{2,1,0:T(8,128)(2,1)S(1)}, u32[]{:S(2)}, u32[]{:S(2)}) async-start(bf16[4,192,256]{2,1,0:T(8,128)(2,1)} %shard_map.119), calls=%async_computation | async-start | bytes 786432 | tf_op jit(solution)/shard_map/all_to_all | solution.py:23
  13.3 6.8 %all-gather = bf16[1,4,64,512]{3,2,1,0:T(8,128)(2,1)S(1)} all-gather(bf16[1,4,64,128]{3,2,1,0:T(8,128)(2,1)} %param.10), channel_id=2, replica_groups=mesh['section'=4,'dp'=32,'tensor'=4] {'tensor'}, dimensions={3}, use_global_device_ids=true | all-gather | bytes 327680 | tf_op jit(solution)/shard_map/all_gather | solution.py:314
  20.2 1.2 all-to-all-done
  21.4 0.7 slice.23
  22.2 3.6 %shard_map.121 = bf16[4,512,512]{2,1,0:T(8,128)(2,1)S(1)} custom-call(s32[4]{0:T(128)S(1)} %copy-done.8, bf16[4,64,512]{2,1,0:T(8,128)(2,1)S(1)} %bitcast.36, bf16[4,64,2048]{2,1,0:T(8,128)(2,1)S(1)} %bitcast.38), custom_call_target="tpu_custom_call" | custom-call | flops 536870912 | bytes 3145728 | tf_op jit(solution)/shard_map/pallas_call | solution.py:83
  25.9 1.3 copy-done.2
  27.2 3.6 %all-to-all-start.1 = ((bf16[4,512,512]{2,1,0:T(8,128)(2,1)}), bf16[4,512,512]{2,1,0:T(8,128)(2,1)S(1)}, u32[]{:S(2)}, u32[]{:S(2)}) async-start(bf16[4,512,512]{2,1,0:T(8,128)(2,1)} %copy-done.2), calls=%async_computation.1 | async-start | bytes 4194304 | tf_op jit(solution)/shard_map/all_to_all | solution.py:23
  30.8 2.2 %broadcast_select_fusion.2 = (bf16[256,512]{1,0:T(8,128)(2,1)}, bf16[256,512]{1,0:T(8,128)(2,1)}, bf16[256,512]{1,0:T(8,128)(2,1)}, bf16[256,512]{1,0:T(8,128)(2,1)}) fusion(pred[]{:T(512)S(6)} %or.3, bf16[256,2048]{1,0:T(8,128)(2,1)} %bitcast.44), kind=kLoop, calls=%fused_computation.31 | loop fusion | flops 524288 | bytes 2097153 | tf_op jit(solution)/shard_map/jit(_where)/select_n | solution.py:347
  33.0 0.3 copy.18
  33.3 0.3 reshape.140
  33.7 0.2 slice-done
  33.9 27.2 %all-gather.2 = bf16[32,32,256]{2,1,0:T(8,128)(2,1)S(1)} all-gather(bf16[4,32,256]{2,1,0:T(8,128)(2,1)S(1)} %slice-done), channel_id=4, replica_groups={{0,4,8,12,16,20,24,28},{32,36,40,44,48,52,56,60},{64,68,72,76,80,84,88,..., dimensions={0}, use_global_device_ids=true | all-gather | bytes 589824 | tf_op jit(solution)/shard_map/all_gather | solution.py:329
  61.0 1.1 shard_map.122
  62.1 6.8 %all-to-all-start.2 = ((bf16[8,4,16,512]{3,2,1,0:T(8,128)(2,1)}), bf16[8,4,16,512]{3,2,1,0:T(8,128)(2,1)S(1)}, u32[]{:S(2)}, u32[]{:S(2)}) async-start(bf16[8,4,16,512]{3,2,1,0:T(8,128)(2,1)} %shard_map.122), calls=%async_computation.2 | async-start | bytes 1048576 | tf_op jit(solution)/shard_map/all_to_all | solution.py:23
  68.9 0.7 slice.27
  69.8 1.4 copy-done
  71.2 0.4 shard_map.120
  71.6 1.3 collective-permute-start
  72.9 0.4 shard_map.123
  73.4 0.8 copy-done.4
  74.2 7.1 %all-to-all-done.2.parts = bf16[8,4,16,512]{3,2,1,0:T(8,128)(2,1)S(1)} async-done(((bf16[8,4,16,512]{3,2,1,0:T(8,128)(2,1)}), bf16[8,4,16,512]{3,2,1,0:T(8,128)(2,1)S(1)}, u32[]{:S(2)}, u32[]{:S(2)}) %all-to-all-start.2) | async-done | bytes 524320 | tf_op jit(solution)/shard_map/all_to_all | solution.py:23
  81.3 0.9 shard_map.124
  82.2 3.1 %collective-permute-done = bf16[256,512]{1,0:T(8,128)(2,1)} collective-permute-done((bf16[256,512]{1,0:T(8,128)(2,1)S(1)}, bf16[256,512]{1,0:T(8,128)(2,1)}, u32[]{:S(2)}, u32[]{:S(2)}) %collective-permute-start) | collective-permute-done | bytes 262176 | tf_op jit(solution)/shard_map/ppermute | solution.py:338
  85.3 1.1 fusion
  86.4 1.3 collective-permute-start.1
  87.7 7.2 %all-to-all-start.3 = ((bf16[8,4,16,512]{3,2,1,0:T(8,128)(2,1)}), bf16[8,4,16,512]{3,2,1,0:T(8,128)(2,1)S(1)}, u32[]{:S(2)}, u32[]{:S(2)}) async-start(bf16[8,4,16,512]{3,2,1,0:T(8,128)(2,1)} %shard_map.124), calls=%async_computation.3 | async-start | bytes 1048576 | tf_op jit(solution)/shard_map/all_to_all | solution.py:23
  94.9 1.3 collective-permute-start.2
  96.2 0.7 collective-permute-done.1
  96.9 1.9 %fusion.5 = bf16[256,512]{1,0:T(8,128)(2,1)} fusion(bf16[256,512]{1,0:T(8,128)(2,1)S(1)} %collective-permute-done.1, bf16[256,512]{1,0:T(8,128)(2,1)S(1)} %fusion, f32[256,512]{1,0:T(8,128)S(1)} %get-tuple-element.53, bf16[256,512]{1,0:T(8,128)(2,1)} %collective-permute-done, pred[]{:T(512)S(6)} %eq.10, pred[]{:T(512)S(6)} %eq.13), kind=kLoop, calls=%fused_computation.22 | loop fusion | flops 917504 | bytes 1572866 | tf_op jit(solution)/shard_map/jit(_where)/select_n | solution.py:363
  98.8 8.1 %collective-permute-done.2 = bf16[256,512]{1,0:T(8,128)(2,1)} collective-permute-done((bf16[256,512]{1,0:T(8,128)(2,1)S(1)}, bf16[256,512]{1,0:T(8,128)(2,1)}, u32[]{:S(2)}, u32[]{:S(2)}) %collective-permute-start.2) | collective-permute-done | bytes 262176 | tf_op jit(solution)/shard_map/ppermute | solution.py:382
  106.9 1.1 fusion.2
  108.0 1.3 collective-permute-start.3
  109.3 1.9 %collective-permute-start.4 = (bf16[256,512]{1,0:T(8,128)(2,1)}, bf16[256,512]{1,0:T(8,128)(2,1)}, u32[]{:S(2)}, u32[]{:S(2)}) collective-permute-start(bf16[256,512]{1,0:T(8,128)(2,1)} %fusion.5), channel_id=1, source_target_pairs={{128,0},{0,128},{384,256},{129,1},{1,129},{385,257},{130,2},{2,130... | collective-permute-start | bytes 786440 | tf_op jit(solution)/shard_map/ppermute | solution.py:386
  111.2 3.5 %all-to-all-done.3.block = bf16[8,4,16,512]{3,2,1,0:T(8,128)(2,1)S(1)} async-done(((bf16[8,4,16,512]{3,2,1,0:T(8,128)(2,1)}), bf16[8,4,16,512]{3,2,1,0:T(8,128)(2,1)S(1)}, u32[]{:S(2)}, u32[]{:S(2)}) %all-to-all-start.3) | async-done | bytes 524320 | tf_op jit(solution)/shard_map/all_to_all | solution.py:23
  114.8 6.9 %all-gather.9.cloned.1.call-done = bf16[32,64,256]{2,1,0:T(8,128)(2,1)} async-done(((bf16[4,64,256]{2,1,0:T(8,128)(2,1)}), bf16[32,64,256]{2,1,0:T(8,128)(2,1)}) %all-gather.9.cloned.1.call-update) | async-done | bytes 1048592 | tf_op jit(solution)/shard_map/all_gather | solution.py:324
  121.7 1.2 copy-done.1
  122.9 3.7 %shard_map.125 = bf16[4,5,16,512]{3,2,1,0:T(8,128)(2,1)} custom-call(s32[1]{0:T(128)} %bitcast.11.y_ref, bf16[8,4,64,256]{3,2,1,0:T(8,128)(2,1)S(1)} %bitcast.30, bf16[8,4,64,256]{3,2,1,0:T(8,128)(2,1)S(1)} %bitcast.31, bf16[8,4,64,256]{3,2,1,0:T(8,128)(2,1)S(1)} %bitcast.32, bf16[8,4,64,256]{3,2,1,0:T(8,128)(2,1)S(1)} %bitcast.33, ...), custom_call_target="tpu_custom_call" | custom-call | flops 805306368 | bytes 2097152 | tf_op jit(solution)/shard_map/pallas_call | solution.py:246
  126.6 2.0 %fusion.7 = bf16[256,512]{1,0:T(8,128)(2,1)} fusion(bf16[256,512]{1,0:T(8,128)(2,1)} %collective-permute-done.3, bf16[256,512]{1,0:T(8,128)(2,1)S(1)} %fusion.2, f32[256,512]{1,0:T(8,128)S(1)} %get-tuple-element.56, bf16[256,512]{1,0:T(8,128)(2,1)} %collective-permute-done.2, pred[]{:T(512)S(6)} %eq.10, pred[]{:T(512)S(6)} %eq.13), kind=kLoop, calls=%fused_computation.24 | loop fusion | flops 917504 | bytes 1572866 | tf_op jit(solution)/shard_map/jit(_where)/select_n | solution.py:363
  128.7 3.6 %collective-permute-start.5 = (bf16[256,512]{1,0:T(8,128)(2,1)}, bf16[256,512]{1,0:T(8,128)(2,1)}, u32[]{:S(2)}, u32[]{:S(2)}) collective-permute-start(bf16[256,512]{1,0:T(8,128)(2,1)} %fusion.7), channel_id=1, source_target_pairs={{128,0},{0,128},{384,256},{129,1},{1,129},{385,257},{130,2},{2,130... | collective-permute-start | bytes 786440 | tf_op jit(solution)/shard_map/ppermute | solution.py:397
  132.3 3.5 %all-to-all-start.4 = ((bf16[4,5,16,512]{3,2,1,0:T(8,128)(2,1)}), bf16[4,5,16,512]{3,2,1,0:T(8,128)(2,1)S(1)}, u32[]{:S(2)}, u32[]{:S(2)}) async-start(bf16[4,5,16,512]{3,2,1,0:T(8,128)(2,1)} %shard_map.125), calls=%async_computation.4 | async-start | bytes 655360 | tf_op jit(solution)/shard_map/all_to_all | solution.py:23
  135.8 2.4 %fusion.9 = (bf16[256,512]{1,0:T(8,128)(2,1)}, bf16[256,512]{1,0:T(8,128)(2,1)}) fusion(bf16[256,512]{1,0:T(8,128)(2,1)} %copy-done.12, f32[256,512]{1,0:T(8,128)S(1)} %get-tuple-element.53, bf16[256,512]{1,0:T(8,128)(2,1)} %collective-permute-done, bf16[256,512]{1,0:T(8,128)(2,1)} %copy-done.18, bf16[256,512]{1,0:T(8,128)(2,1)S(1)} %copy-done.11, ...), kind=kLoop, calls=%fused_computation.26 | loop fusion | flops 2621440 | bytes 3670018 | tf_op jit(solution)/shard_map/jit(_where)/select_n | solution.py:369
  138.2 4.5 %all-to-all-done.4.back = bf16[4,5,16,512]{3,2,1,0:T(8,128)(2,1)S(1)} async-done(((bf16[4,5,16,512]{3,2,1,0:T(8,128)(2,1)}), bf16[4,5,16,512]{3,2,1,0:T(8,128)(2,1)S(1)}, u32[]{:S(2)}, u32[]{:S(2)}) %all-to-all-start.4) | async-done | bytes 327712 | tf_op jit(solution)/shard_map/all_to_all | solution.py:23
  142.8 1.4 shard_map.126
  144.1 1.1 fusion.12
  145.2 1.1 fusion.13
  146.3 0.2 broadcast_select_fusion.1
  146.5 1.1 pad_maximum_fusion
  (46 shorter events, 0.3 us)
Async XLA Ops:
  7.2 15.0 %copy-start.3 = (bf16[1,4,64,2048]{3,2,1,0:T(8,128)(2,1)S(1)}, bf16[1,4,64,2048]{3,2,1,0:T(8,128)(2,1)}, u32[]{:S(2)}) copy-start(bf16[1,4,64,2048]{3,2,1,0:T(8,128)(2,1)} %param.9) | copy-start | bytes 3145732
  7.2 15.0 %copy-start.8 = (s32[4]{0:T(128)S(1)}, s32[4]{0:T(128)}, u32[]{:S(2)}) copy-start(s32[4]{0:T(128)} %order.1) | copy-start | bytes 52
  9.0 12.4 %all-to-all-start = ((bf16[4,192,256]{2,1,0:T(8,128)(2,1)}), bf16[4,192,256]{2,1,0:T(8,128)(2,1)S(1)}, u32[]{:S(2)}, u32[]{:S(2)}) async-start(bf16[4,192,256]{2,1,0:T(8,128)(2,1)} %shard_map.119), calls=%async_computation | async-start | bytes 786432 | tf_op jit(solution)/shard_map/all_to_all | solution.py:23
  13.3 56.2 %all-gather.7.cloned.1.call-start = ((), (), s32[]{:S(2)}) async-start(), calls=%async_computation.5 | async-start | bytes 1769472 | tf_op jit(solution)/shard_map/all_gather | solution.py:322
  21.4 11.6 %copy-start.14 = (bf16[4,192,256]{2,1,0:T(8,128)(2,1)}, bf16[4,192,256]{2,1,0:T(8,128)(2,1)S(1)}, u32[]{:S(2)}) copy-start(bf16[4,192,256]{2,1,0:T(8,128)(2,1)S(1)} %all-to-all-done) | copy-start | bytes 1179652
  25.8 1.3 copy-start.2
  27.2 33.8 %all-to-all-start.1 = ((bf16[4,512,512]{2,1,0:T(8,128)(2,1)}), bf16[4,512,512]{2,1,0:T(8,128)(2,1)S(1)}, u32[]{:S(2)}, u32[]{:S(2)}) async-start(bf16[4,512,512]{2,1,0:T(8,128)(2,1)} %copy-done.2), calls=%async_computation.1 | async-start | bytes 4194304 | tf_op jit(solution)/shard_map/all_to_all | solution.py:23
  33.0 0.8 slice-start
  33.9 35.0 %copy-start.15 = (bf16[4,192,256]{2,1,0:T(8,128)(2,1)S(1)}, bf16[4,192,256]{2,1,0:T(8,128)(2,1)}, u32[]{:S(2)}) copy-start(bf16[4,192,256]{2,1,0:T(8,128)(2,1)} %copy-done.14) | copy-start | bytes 1179652
  62.1 19.2 %all-to-all-start.2 = ((bf16[8,4,16,512]{3,2,1,0:T(8,128)(2,1)}), bf16[8,4,16,512]{3,2,1,0:T(8,128)(2,1)S(1)}, u32[]{:S(2)}, u32[]{:S(2)}) async-start(bf16[8,4,16,512]{3,2,1,0:T(8,128)(2,1)} %shard_map.122), calls=%async_computation.2 | async-start | bytes 1048576 | tf_op jit(solution)/shard_map/all_to_all | solution.py:23
  68.9 52.8 %all-gather.9.cloned.1.call-start = ((), (), s32[]{:S(2)}) async-start(), calls=%async_computation.6 | async-start | bytes 1179648 | tf_op jit(solution)/shard_map/all_gather | solution.py:324
  69.8 1.4 copy-start
  71.6 13.6 %collective-permute-start = (bf16[256,512]{1,0:T(8,128)(2,1)S(1)}, bf16[256,512]{1,0:T(8,128)(2,1)}, u32[]{:S(2)}, u32[]{:S(2)}) collective-permute-start(bf16[256,512]{1,0:T(8,128)(2,1)S(1)} %get-tuple-element.38), channel_id=1, source_target_pairs={{384,256},{256,384},{128,0},{385,257},{257,385},{129,1},{386,258},... | collective-permute-start | bytes 786440 | tf_op jit(solution)/shard_map/ppermute | solution.py:338
  73.4 0.8 copy-start.4
  82.2 24.7 %copy-start.10 = (bf16[256,512]{1,0:T(8,128)(2,1)S(1)}, bf16[256,512]{1,0:T(8,128)(2,1)}, u32[]{:S(2)}) copy-start(bf16[256,512]{1,0:T(8,128)(2,1)} %get-tuple-element.68) | copy-start | bytes 786436
  86.4 45.9 %copy-start.12 = (bf16[256,512]{1,0:T(8,128)(2,1)}, bf16[256,512]{1,0:T(8,128)(2,1)S(1)}, u32[]{:S(2)}) copy-start(bf16[256,512]{1,0:T(8,128)(2,1)S(1)} %fusion) | copy-start | bytes 786436
  86.4 10.5 %collective-permute-start.1 = (bf16[256,512]{1,0:T(8,128)(2,1)S(1)}, bf16[256,512]{1,0:T(8,128)(2,1)S(1)}, u32[]{:S(2)}, u32[]{:S(2)}) collective-permute-start(bf16[256,512]{1,0:T(8,128)(2,1)S(1)} %fusion), channel_id=1, source_target_pairs={{256,128},{384,0},{257,129},{385,1},{258,130},{386,2},{259,131},{3... | collective-permute-start | bytes 786440 | tf_op jit(solution)/shard_map/ppermute | solution.py:379
  87.7 27.1 %all-to-all-start.3 = ((bf16[8,4,16,512]{3,2,1,0:T(8,128)(2,1)}), bf16[8,4,16,512]{3,2,1,0:T(8,128)(2,1)S(1)}, u32[]{:S(2)}, u32[]{:S(2)}) async-start(bf16[8,4,16,512]{3,2,1,0:T(8,128)(2,1)} %shard_map.124), calls=%async_computation.3 | async-start | bytes 1048576 | tf_op jit(solution)/shard_map/all_to_all | solution.py:23
  94.9 12.0 %collective-permute-start.2 = (bf16[256,512]{1,0:T(8,128)(2,1)S(1)}, bf16[256,512]{1,0:T(8,128)(2,1)}, u32[]{:S(2)}, u32[]{:S(2)}) collective-permute-start(bf16[256,512]{1,0:T(8,128)(2,1)S(1)} %get-tuple-element.48), channel_id=1, source_target_pairs={{384,256},{256,384},{128,0},{385,257},{257,385},{129,1},{386,258},... | collective-permute-start | bytes 786440 | tf_op jit(solution)/shard_map/ppermute | solution.py:382
  96.9 24.8 %copy-start.18 = (bf16[256,512]{1,0:T(8,128)(2,1)}, bf16[256,512]{1,0:T(8,128)(2,1)S(1)}, u32[]{:S(2)}) copy-start(bf16[256,512]{1,0:T(8,128)(2,1)S(1)} %collective-permute-done.1) | copy-start | bytes 786436
  108.0 18.7 %copy-start.13 = (bf16[256,512]{1,0:T(8,128)(2,1)}, bf16[256,512]{1,0:T(8,128)(2,1)S(1)}, u32[]{:S(2)}) copy-start(bf16[256,512]{1,0:T(8,128)(2,1)S(1)} %fusion.2) | copy-start | bytes 786436
  108.0 18.6 %collective-permute-start.3 = (bf16[256,512]{1,0:T(8,128)(2,1)S(1)}, bf16[256,512]{1,0:T(8,128)(2,1)}, u32[]{:S(2)}, u32[]{:S(2)}) collective-permute-start(bf16[256,512]{1,0:T(8,128)(2,1)S(1)} %fusion.2), channel_id=1, source_target_pairs={{256,128},{384,0},{257,129},{385,1},{258,130},{386,2},{259,131},{3... | collective-permute-start | bytes 786440 | tf_op jit(solution)/shard_map/ppermute | solution.py:390
  109.3 34.8 %collective-permute-start.4 = (bf16[256,512]{1,0:T(8,128)(2,1)}, bf16[256,512]{1,0:T(8,128)(2,1)}, u32[]{:S(2)}, u32[]{:S(2)}) collective-permute-start(bf16[256,512]{1,0:T(8,128)(2,1)} %fusion.5), channel_id=1, source_target_pairs={{128,0},{0,128},{384,256},{129,1},{1,129},{385,257},{130,2},{2,130... | collective-permute-start | bytes 786440 | tf_op jit(solution)/shard_map/ppermute | solution.py:386
  121.7 1.2 copy-start.1
  126.6 9.1 %copy-start.11 = (bf16[256,512]{1,0:T(8,128)(2,1)S(1)}, bf16[256,512]{1,0:T(8,128)(2,1)}, u32[]{:S(2)}) copy-start(bf16[256,512]{1,0:T(8,128)(2,1)} %get-tuple-element.70) | copy-start | bytes 786436
  128.7 14.1 %copy-start.6 = (f32[1,4,16,512]{3,2,1,0:T(8,128)S(1)}, f32[1,4,16,512]{3,2,1,0:T(8,128)}, u32[]{:S(2)}) copy-start(f32[1,4,16,512]{3,2,1,0:T(8,128)} %param.12) | copy-start | bytes 393220
  128.7 14.1 %copy-start.7 = (f32[1,4,16,512]{3,2,1,0:T(8,128)S(1)}, f32[1,4,16,512]{3,2,1,0:T(8,128)}, u32[]{:S(2)}) copy-start(f32[1,4,16,512]{3,2,1,0:T(8,128)} %param.13) | copy-start | bytes 393220
  128.7 14.1 %copy-start.9 = (s32[1,1,2]{2,1,0:T(1,128)S(1)}, s32[1,1,2]{2,1,0:T(1,128)}, u32[]{:S(2)}) copy-start(s32[1,1,2]{2,1,0:T(1,128)} %param.14) | copy-start | bytes 28
  128.7 15.4 %collective-permute-start.5 = (bf16[256,512]{1,0:T(8,128)(2,1)}, bf16[256,512]{1,0:T(8,128)(2,1)}, u32[]{:S(2)}, u32[]{:S(2)}) collective-permute-start(bf16[256,512]{1,0:T(8,128)(2,1)} %fusion.7), channel_id=1, source_target_pairs={{128,0},{0,128},{384,256},{129,1},{1,129},{385,257},{130,2},{2,130... | collective-permute-start | bytes 786440 | tf_op jit(solution)/shard_map/ppermute | solution.py:397
  132.3 10.5 %all-to-all-start.4 = ((bf16[4,5,16,512]{3,2,1,0:T(8,128)(2,1)}), bf16[4,5,16,512]{3,2,1,0:T(8,128)(2,1)S(1)}, u32[]{:S(2)}, u32[]{:S(2)}) async-start(bf16[4,5,16,512]{3,2,1,0:T(8,128)(2,1)} %shard_map.125), calls=%async_computation.4 | async-start | bytes 655360 | tf_op jit(solution)/shard_map/all_to_all | solution.py:23
  135.8 9.4 %copy-start.5 = (f32[256,512]{1,0:T(8,128)S(1)}, f32[256,512]{1,0:T(8,128)}, u32[]{:S(2)}) copy-start(f32[256,512]{1,0:T(8,128)} %copy-done.4) | copy-start | bytes 1572868
  138.2 8.1 %copy-start.16 = (bf16[256,512]{1,0:T(8,128)(2,1)S(1)}, bf16[256,512]{1,0:T(8,128)(2,1)}, u32[]{:S(2)}) copy-start(bf16[256,512]{1,0:T(8,128)(2,1)} %get-tuple-element.71) | copy-start | bytes 786436
  138.2 8.1 %copy-start.17 = (bf16[256,512]{1,0:T(8,128)(2,1)S(1)}, bf16[256,512]{1,0:T(8,128)(2,1)}, u32[]{:S(2)}) copy-start(bf16[256,512]{1,0:T(8,128)(2,1)} %get-tuple-element.72) | copy-start | bytes 786436
Sparse Core Ops, SparseCore 0:
  22.3 47.1 all-gather.6
  72.4 49.2 all-gather.8

commit v5 on v4

--- a/solution.py
+++ b/solution.py
@@ -1,5 +1,3 @@
-import functools
-
 import jax
 import jax.numpy as jnp
 from jax import lax
@@ -187,16 +185,19 @@
     )(half.reshape(1).astype(jnp.int32), values, *arrays, *arrays)
 
 
-def solve_kernel(y_ref, left_0, left_1, right_0, right_1, block, sent, rows, left, right, matrix):
+def solve_kernel(y_ref, stats, block, sent, rows, left, right, matrix):
     own, size = block.shape[2:]
     y = y_ref[0]
     for x in range(NX):
         for other in range(NY):
             place = slice((x * NY + other) * own, (x * NY + other + 1) * own)
             rows[place, :] = block[other, x]
-            for ref, pieces in ((left, (left_0, left_1)), (right, (right_0, right_1))):
-                for p, piece in enumerate(pieces):
-                    ref[place, p * PIECE : (p + 1) * PIECE] = piece[other, x].astype(jnp.float32)
+            for side, ref in enumerate((left, right)):
+                for p in range(size // PIECE):
+                    group = side * (size // PIECE) + p
+                    ref[place, p * PIECE : (p + 1) * PIECE] = stats[
+                        other, x, group * own : (group + 1) * own, :
+                    ].astype(jnp.float32)
     whole = rows[...]
     starts = [pl.multiple_of(x * NY * own + y * own, own) for x in range(NX)]
 
@@ -237,24 +238,13 @@
             sent[x, 3 + side] = root[part]
 
 
-def group_place(group, i):
-    return 0, 0, group, 0
-
-
 def solve(y_index, gathered, block):
     own, size = block.shape[2:]
+    vmem = pl.BlockSpec(memory_space=pltpu.VMEM)
     return pl.pallas_call(
         solve_kernel,
-        grid=(1,),
-        in_specs=[
-            pl.BlockSpec(memory_space=pltpu.SMEM),
-            *[
-                pl.BlockSpec((NY, NX, own, PIECE), functools.partial(group_place, g))
-                for g in range(4)
-            ],
-            pl.BlockSpec(block.shape, lambda i: (0, 0, 0, 0)),
-        ],
-        out_specs=pl.BlockSpec((NX, 5, own, size), lambda i: (0, 0, 0, 0)),
+        in_specs=[pl.BlockSpec(memory_space=pltpu.SMEM), vmem, vmem],
+        out_specs=vmem,
         out_shape=jax.ShapeDtypeStruct((NX, 5, own, size), jnp.bfloat16),
         scratch_shapes=[
             pltpu.VMEM((size, size), jnp.bfloat16),
@@ -266,7 +256,7 @@
             flops=3 * 2 * size**3, bytes_accessed=2 * 1024 * 1024, transcendentals=0
         ),
         compiler_params=PARAMS,
-    )(y_index.reshape(1).astype(jnp.int32), *[gathered] * 4, block)
+    )(y_index.reshape(1).astype(jnp.int32), gathered, block)
 
 
 def finish_kernel(refresh, back, left_stats, right_stats, weight_grad, new_left, new_right, roots):

time: 155 us -> 155 us (level)
    unnamed x38 -> x42, local copies, waits for them, and re-layouts: 4.8 us -> 4.82 us
where the time goes in v5:
time: 155 us; the launch traced here: 154 us
  starting transfers between devices  35.9 us (23%)
  waiting for transfers between devices  35.4 us (23%)
  blocking collectives  34.1 us (22%)
  between operations  14.3 us (9%)
  other arithmetic  14 us (9%)
  Pallas kernels  13.5 us (9%)
  local copies, waits for them, and re-layouts  7.2 us (5%)
    all_gather x1, blocking collectives, per_device(): last = lax.all_gather(last, 'dp', axis=0, axis_index_groups=Y_GROUPS)  27.3 us
    all_to_all x5, starting transfers between devices, exchange(): lax.all_to_all(block, 'dp', 0, 0, axis_index_groups=groups, tiled=True)  25.2 us
    all_to_all x5, waiting for transfers between devices, exchange(): lax.all_to_all(block, 'dp', 0, 0, axis_index_groups=groups, tiled=True)  16.9 us
    ppermute x1, waiting for transfers between devices, per_device(): mates.append(lax.ppermute(far_1, 'section', to_mate))  7.54 us
    all_gather x1, blocking collectives, per_device(): value_full = lax.all_gather(value_grad[0], 'tensor', axis=2, tiled=True)  6.84 us
    all_gather x1, waiting for transfers between devices, per_device(): stats = lax.all_gather(stats, 'dp', axis=0, axis_index_groups=Y_GROUPS)  6.73 us
    unnamed x42, local copies, waits for them, and re-layouts  4.82 us
    select_n x2, other arithmetic, forward(): jnp.where(section == 0, second, jnp.where(section == 1, updated, held))  3.93 us
  transfers between devices with their start and end apart: 13, of which 8 were waited for; matrix products, arithmetic and copies ran while one was open for 8% of the time, Pallas kernels for 8%

profile of v5, /device:TPU:8, one launch (start us, length us, event | category | flops | bytes accessed | tf_op | source)
XLA Modules:
  0.0 154.4 jit_solution(13782286726910701894)
XLA Ops:
  7.2 1.9 %shard_map.119 = bf16[4,192,256]{2,1,0:T(8,128)(2,1)} custom-call(bf16[16,2048]{1,0:T(8,128)(2,1)} %bitcast.48, f32[4,16,512]{2,1,0:T(8,128)} %bitcast.35, f32[4,16,512]{2,1,0:T(8,128)} %bitcast.37), custom_call_target="tpu_custom_call" | custom-call | flops 1024 | bytes 1048576 | tf_op jit(solution)/shard_map/pallas_call | solution.py:49
  9.0 4.3 %all-to-all-start = ((bf16[4,192,256]{2,1,0:T(8,128)(2,1)}), bf16[4,192,256]{2,1,0:T(8,128)(2,1)S(1)}, u32[]{:S(2)}, u32[]{:S(2)}) async-start(bf16[4,192,256]{2,1,0:T(8,128)(2,1)} %shard_map.119), calls=%async_computation | async-start | bytes 786432 | tf_op jit(solution)/shard_map/all_to_all | solution.py:21
  13.3 6.8 %all-gather = bf16[1,4,64,512]{3,2,1,0:T(8,128)(2,1)S(1)} all-gather(bf16[1,4,64,128]{3,2,1,0:T(8,128)(2,1)} %param.10), channel_id=2, replica_groups=mesh['section'=4,'dp'=32,'tensor'=4] {'tensor'}, dimensions={3}, use_global_device_ids=true | all-gather | bytes 327680 | tf_op jit(solution)/shard_map/all_gather | solution.py:304
  20.2 1.2 all-to-all-done
  21.4 0.8 slice.23
  22.2 3.6 %shard_map.121 = bf16[4,512,512]{2,1,0:T(8,128)(2,1)S(1)} custom-call(s32[4]{0:T(128)S(1)} %copy-done.7, bf16[4,64,512]{2,1,0:T(8,128)(2,1)S(1)} %bitcast.32, bf16[4,64,2048]{2,1,0:T(8,128)(2,1)S(1)} %bitcast.34), custom_call_target="tpu_custom_call" | custom-call | flops 536870912 | bytes 3145728 | tf_op jit(solution)/shard_map/pallas_call | solution.py:81
  25.9 1.3 copy-done.1
  27.2 3.6 %all-to-all-start.1 = ((bf16[4,512,512]{2,1,0:T(8,128)(2,1)}), bf16[4,512,512]{2,1,0:T(8,128)(2,1)S(1)}, u32[]{:S(2)}, u32[]{:S(2)}) async-start(bf16[4,512,512]{2,1,0:T(8,128)(2,1)} %copy-done.1), calls=%async_computation.1 | async-start | bytes 4194304 | tf_op jit(solution)/shard_map/all_to_all | solution.py:21
  30.8 2.2 %broadcast_select_fusion.2 = (bf16[256,512]{1,0:T(8,128)(2,1)}, bf16[256,512]{1,0:T(8,128)(2,1)}, bf16[256,512]{1,0:T(8,128)(2,1)}, bf16[256,512]{1,0:T(8,128)(2,1)}) fusion(pred[]{:T(512)S(6)} %or.3, bf16[256,2048]{1,0:T(8,128)(2,1)} %bitcast.41), kind=kLoop, calls=%fused_computation.31 | loop fusion | flops 524288 | bytes 2097153 | tf_op jit(solution)/shard_map/jit(_where)/select_n | solution.py:337
  33.1 0.3 copy.18
  33.4 0.3 reshape.140
  33.7 0.2 slice-done
  33.9 27.3 %all-gather.2 = bf16[32,32,256]{2,1,0:T(8,128)(2,1)S(1)} all-gather(bf16[4,32,256]{2,1,0:T(8,128)(2,1)S(1)} %slice-done), channel_id=4, replica_groups={{0,4,8,12,16,20,24,28},{32,36,40,44,48,52,56,60},{64,68,72,76,80,84,88,..., dimensions={0}, use_global_device_ids=true | all-gather | bytes 589824 | tf_op jit(solution)/shard_map/all_gather | solution.py:319
  61.2 1.1 shard_map.122
  62.2 6.6 %all-to-all-start.2 = ((bf16[8,4,16,512]{3,2,1,0:T(8,128)(2,1)}), bf16[8,4,16,512]{3,2,1,0:T(8,128)(2,1)S(1)}, u32[]{:S(2)}, u32[]{:S(2)}) async-start(bf16[8,4,16,512]{3,2,1,0:T(8,128)(2,1)} %shard_map.122), calls=%async_computation.2 | async-start | bytes 1048576 | tf_op jit(solution)/shard_map/all_to_all | solution.py:21
  68.9 0.7 slice.27
  69.8 1.4 copy-done
  71.2 0.4 shard_map.120
  71.6 1.3 collective-permute-start
  72.9 0.4 shard_map.123
  73.4 0.8 copy-done.3
  74.2 7.2 %all-to-all-done.2.parts = bf16[8,4,16,512]{3,2,1,0:T(8,128)(2,1)S(1)} async-done(((bf16[8,4,16,512]{3,2,1,0:T(8,128)(2,1)}), bf16[8,4,16,512]{3,2,1,0:T(8,128)(2,1)S(1)}, u32[]{:S(2)}, u32[]{:S(2)}) %all-to-all-start.2) | async-done | bytes 524320 | tf_op jit(solution)/shard_map/all_to_all | solution.py:21
  81.4 0.9 shard_map.124
  82.3 3.0 %collective-permute-done = bf16[256,512]{1,0:T(8,128)(2,1)} collective-permute-done((bf16[256,512]{1,0:T(8,128)(2,1)S(1)}, bf16[256,512]{1,0:T(8,128)(2,1)}, u32[]{:S(2)}, u32[]{:S(2)}) %collective-permute-start) | collective-permute-done | bytes 262176 | tf_op jit(solution)/shard_map/ppermute | solution.py:328
  85.3 1.1 fusion
  86.5 1.3 collective-permute-start.1
  87.8 7.2 %all-to-all-start.3 = ((bf16[8,4,16,512]{3,2,1,0:T(8,128)(2,1)}), bf16[8,4,16,512]{3,2,1,0:T(8,128)(2,1)S(1)}, u32[]{:S(2)}, u32[]{:S(2)}) async-start(bf16[8,4,16,512]{3,2,1,0:T(8,128)(2,1)} %shard_map.124), calls=%async_computation.3 | async-start | bytes 1048576 | tf_op jit(solution)/shard_map/all_to_all | solution.py:21
  95.0 1.3 collective-permute-start.2
  96.3 1.1 collective-permute-done.1
  97.4 1.9 %fusion.5 = bf16[256,512]{1,0:T(8,128)(2,1)} fusion(bf16[256,512]{1,0:T(8,128)(2,1)S(1)} %collective-permute-done.1, bf16[256,512]{1,0:T(8,128)(2,1)S(1)} %fusion, f32[256,512]{1,0:T(8,128)S(1)} %get-tuple-element.53, bf16[256,512]{1,0:T(8,128)(2,1)} %collective-permute-done, pred[]{:T(512)S(6)} %eq.10, pred[]{:T(512)S(6)} %eq.13), kind=kLoop, calls=%fused_computation.22 | loop fusion | flops 917504 | bytes 1572866 | tf_op jit(solution)/shard_map/jit(_where)/select_n | solution.py:353
  99.3 7.5 %collective-permute-done.2 = bf16[256,512]{1,0:T(8,128)(2,1)S(1)} collective-permute-done((bf16[256,512]{1,0:T(8,128)(2,1)S(1)}, bf16[256,512]{1,0:T(8,128)(2,1)S(1)}, u32[]{:S(2)}, u32[]{:S(2)}) %collective-permute-start.2) | collective-permute-done | bytes 262176 | tf_op jit(solution)/shard_map/ppermute | solution.py:372
  106.8 0.8 fusion.2
  107.7 1.3 collective-permute-start.3
  109.0 1.9 %collective-permute-start.4 = (bf16[256,512]{1,0:T(8,128)(2,1)}, bf16[256,512]{1,0:T(8,128)(2,1)}, u32[]{:S(2)}, u32[]{:S(2)}) collective-permute-start(bf16[256,512]{1,0:T(8,128)(2,1)} %fusion.5), channel_id=1, source_target_pairs={{128,0},{0,128},{384,256},{129,1},{1,129},{385,257},{130,2},{2,130... | collective-permute-start | bytes 786440 | tf_op jit(solution)/shard_map/ppermute | solution.py:376
  110.9 3.9 %all-to-all-done.3.block = bf16[8,4,16,512]{3,2,1,0:T(8,128)(2,1)S(1)} async-done(((bf16[8,4,16,512]{3,2,1,0:T(8,128)(2,1)}), bf16[8,4,16,512]{3,2,1,0:T(8,128)(2,1)S(1)}, u32[]{:S(2)}, u32[]{:S(2)}) %all-to-all-start.3) | async-done | bytes 524320 | tf_op jit(solution)/shard_map/all_to_all | solution.py:21
  114.8 6.7 %all-gather.9.cloned.1.call-done = bf16[32,64,256]{2,1,0:T(8,128)(2,1)} async-done(((bf16[4,64,256]{2,1,0:T(8,128)(2,1)}), bf16[32,64,256]{2,1,0:T(8,128)(2,1)}) %all-gather.9.cloned.1.call-update) | async-done | bytes 1048592 | tf_op jit(solution)/shard_map/all_gather | solution.py:314
  121.6 1.2 copy-done.9
  122.8 3.8 %shard_map.125 = bf16[4,5,16,512]{3,2,1,0:T(8,128)(2,1)} custom-call(s32[1]{0:T(128)} %bitcast.11.y_ref, bf16[8,4,64,256]{3,2,1,0:T(8,128)(2,1)S(1)} %bitcast.40, bf16[8,4,16,512]{3,2,1,0:T(8,128)(2,1)S(1)} %all-to-all-done.3.block), custom_call_target="tpu_custom_call" | custom-call | flops 805306368 | bytes 2097152 | tf_op jit(solution)/shard_map/pallas_call | solution.py:244
  126.6 2.0 %fusion.7 = bf16[256,512]{1,0:T(8,128)(2,1)} fusion(bf16[256,512]{1,0:T(8,128)(2,1)} %collective-permute-done.3, bf16[256,512]{1,0:T(8,128)(2,1)} %fusion.2, f32[256,512]{1,0:T(8,128)S(1)} %get-tuple-element.56, bf16[256,512]{1,0:T(8,128)(2,1)S(1)} %copy-done.15, pred[]{:T(512)S(6)} %eq.10, pred[]{:T(512)S(6)} %eq.13), kind=kLoop, calls=%fused_computation.24 | loop fusion | flops 917504 | bytes 1572866 | tf_op jit(solution)/shard_map/jit(_where)/select_n | solution.py:353
  128.6 3.6 %collective-permute-start.5 = (bf16[256,512]{1,0:T(8,128)(2,1)}, bf16[256,512]{1,0:T(8,128)(2,1)}, u32[]{:S(2)}, u32[]{:S(2)}) collective-permute-start(bf16[256,512]{1,0:T(8,128)(2,1)} %fusion.7), channel_id=1, source_target_pairs={{128,0},{0,128},{384,256},{129,1},{1,129},{385,257},{130,2},{2,130... | collective-permute-start | bytes 786440 | tf_op jit(solution)/shard_map/ppermute | solution.py:387
  132.2 3.5 %all-to-all-start.4 = ((bf16[4,5,16,512]{3,2,1,0:T(8,128)(2,1)}), bf16[4,5,16,512]{3,2,1,0:T(8,128)(2,1)S(1)}, u32[]{:S(2)}, u32[]{:S(2)}) async-start(bf16[4,5,16,512]{3,2,1,0:T(8,128)(2,1)} %shard_map.125), calls=%async_computation.4 | async-start | bytes 655360 | tf_op jit(solution)/shard_map/all_to_all | solution.py:21
  135.7 2.4 %fusion.9 = (bf16[256,512]{1,0:T(8,128)(2,1)}, bf16[256,512]{1,0:T(8,128)(2,1)}) fusion(bf16[256,512]{1,0:T(8,128)(2,1)} %copy-done.13, f32[256,512]{1,0:T(8,128)S(1)} %get-tuple-element.53, bf16[256,512]{1,0:T(8,128)(2,1)} %collective-permute-done, bf16[256,512]{1,0:T(8,128)(2,1)} %copy-done.20, bf16[256,512]{1,0:T(8,128)(2,1)S(1)} %copy-done.12, ...), kind=kLoop, calls=%fused_computation.26 | loop fusion | flops 2621440 | bytes 3670018 | tf_op jit(solution)/shard_map/jit(_where)/select_n | solution.py:359
  138.2 4.5 %all-to-all-done.4.back = bf16[4,5,16,512]{3,2,1,0:T(8,128)(2,1)S(1)} async-done(((bf16[4,5,16,512]{3,2,1,0:T(8,128)(2,1)}), bf16[4,5,16,512]{3,2,1,0:T(8,128)(2,1)S(1)}, u32[]{:S(2)}, u32[]{:S(2)}) %all-to-all-start.4) | async-done | bytes 327712 | tf_op jit(solution)/shard_map/all_to_all | solution.py:21
  142.7 1.4 shard_map.126
  144.1 1.1 fusion.12
  145.2 1.1 fusion.13
  146.2 0.2 broadcast_select_fusion.1
  146.5 1.1 pad_maximum_fusion
  (50 shorter events, 0.3 us)
Async XLA Ops:
  7.2 15.0 %copy-start.2 = (bf16[1,4,64,2048]{3,2,1,0:T(8,128)(2,1)S(1)}, bf16[1,4,64,2048]{3,2,1,0:T(8,128)(2,1)}, u32[]{:S(2)}) copy-start(bf16[1,4,64,2048]{3,2,1,0:T(8,128)(2,1)} %param.9) | copy-start | bytes 3145732
  7.2 15.0 %copy-start.7 = (s32[4]{0:T(128)S(1)}, s32[4]{0:T(128)}, u32[]{:S(2)}) copy-start(s32[4]{0:T(128)} %order.1) | copy-start | bytes 52
  9.0 12.4 %all-to-all-start = ((bf16[4,192,256]{2,1,0:T(8,128)(2,1)}), bf16[4,192,256]{2,1,0:T(8,128)(2,1)S(1)}, u32[]{:S(2)}, u32[]{:S(2)}) async-start(bf16[4,192,256]{2,1,0:T(8,128)(2,1)} %shard_map.119), calls=%async_computation | async-start | bytes 786432 | tf_op jit(solution)/shard_map/all_to_all | solution.py:21
  13.3 56.2 %all-gather.7.cloned.1.call-start = ((), (), s32[]{:S(2)}) async-start(), calls=%async_computation.5 | async-start | bytes 1769472 | tf_op jit(solution)/shard_map/all_gather | solution.py:312
  21.4 11.6 %copy-start.16 = (bf16[4,192,256]{2,1,0:T(8,128)(2,1)}, bf16[4,192,256]{2,1,0:T(8,128)(2,1)S(1)}, u32[]{:S(2)}) copy-start(bf16[4,192,256]{2,1,0:T(8,128)(2,1)S(1)} %all-to-all-done) | copy-start | bytes 1179652
  25.9 1.3 copy-start.1
  27.2 34.0 %all-to-all-start.1 = ((bf16[4,512,512]{2,1,0:T(8,128)(2,1)}), bf16[4,512,512]{2,1,0:T(8,128)(2,1)S(1)}, u32[]{:S(2)}, u32[]{:S(2)}) async-start(bf16[4,512,512]{2,1,0:T(8,128)(2,1)} %copy-done.1), calls=%async_computation.1 | async-start | bytes 4194304 | tf_op jit(solution)/shard_map/all_to_all | solution.py:21
  33.1 0.8 slice-start
  33.9 35.0 %copy-start.17 = (bf16[4,192,256]{2,1,0:T(8,128)(2,1)S(1)}, bf16[4,192,256]{2,1,0:T(8,128)(2,1)}, u32[]{:S(2)}) copy-start(bf16[4,192,256]{2,1,0:T(8,128)(2,1)} %copy-done.16) | copy-start | bytes 1179652
  62.2 19.1 %all-to-all-start.2 = ((bf16[8,4,16,512]{3,2,1,0:T(8,128)(2,1)}), bf16[8,4,16,512]{3,2,1,0:T(8,128)(2,1)S(1)}, u32[]{:S(2)}, u32[]{:S(2)}) async-start(bf16[8,4,16,512]{3,2,1,0:T(8,128)(2,1)} %shard_map.122), calls=%async_computation.2 | async-start | bytes 1048576 | tf_op jit(solution)/shard_map/all_to_all | solution.py:21
  68.9 52.7 %all-gather.9.cloned.1.call-start = ((), (), s32[]{:S(2)}) async-start(), calls=%async_computation.6 | async-start | bytes 1179648 | tf_op jit(solution)/shard_map/all_gather | solution.py:314
  69.8 1.4 copy-start
  71.6 13.7 %collective-permute-start = (bf16[256,512]{1,0:T(8,128)(2,1)S(1)}, bf16[256,512]{1,0:T(8,128)(2,1)}, u32[]{:S(2)}, u32[]{:S(2)}) collective-permute-start(bf16[256,512]{1,0:T(8,128)(2,1)S(1)} %get-tuple-element.38), channel_id=1, source_target_pairs={{384,256},{256,384},{128,0},{385,257},{257,385},{129,1},{386,258},... | collective-permute-start | bytes 786440 | tf_op jit(solution)/shard_map/ppermute | solution.py:328
  73.4 0.8 copy-start.3
  82.3 24.6 %copy-start.10 = (bf16[256,512]{1,0:T(8,128)(2,1)S(1)}, bf16[256,512]{1,0:T(8,128)(2,1)}, u32[]{:S(2)}) copy-start(bf16[256,512]{1,0:T(8,128)(2,1)} %get-tuple-element.68) | copy-start | bytes 786436
  86.4 35.1 %copy-start.13 = (bf16[256,512]{1,0:T(8,128)(2,1)}, bf16[256,512]{1,0:T(8,128)(2,1)S(1)}, u32[]{:S(2)}) copy-start(bf16[256,512]{1,0:T(8,128)(2,1)S(1)} %fusion) | copy-start | bytes 786436
  86.5 10.9 %collective-permute-start.1 = (bf16[256,512]{1,0:T(8,128)(2,1)S(1)}, bf16[256,512]{1,0:T(8,128)(2,1)S(1)}, u32[]{:S(2)}, u32[]{:S(2)}) collective-permute-start(bf16[256,512]{1,0:T(8,128)(2,1)S(1)} %fusion), channel_id=1, source_target_pairs={{256,128},{384,0},{257,129},{385,1},{258,130},{386,2},{259,131},{3... | collective-permute-start | bytes 786440 | tf_op jit(solution)/shard_map/ppermute | solution.py:369
  87.8 27.1 %all-to-all-start.3 = ((bf16[8,4,16,512]{3,2,1,0:T(8,128)(2,1)}), bf16[8,4,16,512]{3,2,1,0:T(8,128)(2,1)S(1)}, u32[]{:S(2)}, u32[]{:S(2)}) async-start(bf16[8,4,16,512]{3,2,1,0:T(8,128)(2,1)} %shard_map.124), calls=%async_computation.3 | async-start | bytes 1048576 | tf_op jit(solution)/shard_map/all_to_all | solution.py:21
  95.0 11.9 %collective-permute-start.2 = (bf16[256,512]{1,0:T(8,128)(2,1)S(1)}, bf16[256,512]{1,0:T(8,128)(2,1)S(1)}, u32[]{:S(2)}, u32[]{:S(2)}) collective-permute-start(bf16[256,512]{1,0:T(8,128)(2,1)S(1)} %get-tuple-element.48), channel_id=1, source_target_pairs={{384,256},{256,384},{128,0},{385,257},{257,385},{129,1},{386,258},... | collective-permute-start | bytes 786440 | tf_op jit(solution)/shard_map/ppermute | solution.py:372
  97.4 24.2 %copy-start.20 = (bf16[256,512]{1,0:T(8,128)(2,1)}, bf16[256,512]{1,0:T(8,128)(2,1)S(1)}, u32[]{:S(2)}) copy-start(bf16[256,512]{1,0:T(8,128)(2,1)S(1)} %collective-permute-done.1) | copy-start | bytes 786436
  106.8 14.7 %copy-start.14 = (bf16[256,512]{1,0:T(8,128)(2,1)}, bf16[256,512]{1,0:T(8,128)(2,1)S(1)}, u32[]{:S(2)}) copy-start(bf16[256,512]{1,0:T(8,128)(2,1)S(1)} %collective-permute-done.2) | copy-start | bytes 786436
  107.7 18.9 %collective-permute-start.3 = (bf16[256,512]{1,0:T(8,128)(2,1)}, bf16[256,512]{1,0:T(8,128)(2,1)}, u32[]{:S(2)}, u32[]{:S(2)}) collective-permute-start(bf16[256,512]{1,0:T(8,128)(2,1)} %fusion.2), channel_id=1, source_target_pairs={{256,128},{384,0},{257,129},{385,1},{258,130},{386,2},{259,131},{3... | collective-permute-start | bytes 786440 | tf_op jit(solution)/shard_map/ppermute | solution.py:380
  109.0 35.1 %collective-permute-start.4 = (bf16[256,512]{1,0:T(8,128)(2,1)}, bf16[256,512]{1,0:T(8,128)(2,1)}, u32[]{:S(2)}, u32[]{:S(2)}) collective-permute-start(bf16[256,512]{1,0:T(8,128)(2,1)} %fusion.5), channel_id=1, source_target_pairs={{128,0},{0,128},{384,256},{129,1},{1,129},{385,257},{130,2},{2,130... | collective-permute-start | bytes 786440 | tf_op jit(solution)/shard_map/ppermute | solution.py:376
  121.6 1.2 copy-start.9
  122.8 3.8 %copy-start.15 = (bf16[256,512]{1,0:T(8,128)(2,1)S(1)}, bf16[256,512]{1,0:T(8,128)(2,1)}, u32[]{:S(2)}) copy-start(bf16[256,512]{1,0:T(8,128)(2,1)} %copy-done.14) | copy-start | bytes 786436
  122.8 12.9 %copy-start.11 = (bf16[256,512]{1,0:T(8,128)(2,1)S(1)}, bf16[256,512]{1,0:T(8,128)(2,1)}, u32[]{:S(2)}) copy-start(bf16[256,512]{1,0:T(8,128)(2,1)} %get-tuple-element.68) | copy-start | bytes 786436
  126.6 9.2 %copy-start.12 = (bf16[256,512]{1,0:T(8,128)(2,1)S(1)}, bf16[256,512]{1,0:T(8,128)(2,1)}, u32[]{:S(2)}) copy-start(bf16[256,512]{1,0:T(8,128)(2,1)} %get-tuple-element.70) | copy-start | bytes 786436
  128.6 14.1 %copy-start.5 = (f32[1,4,16,512]{3,2,1,0:T(8,128)S(1)}, f32[1,4,16,512]{3,2,1,0:T(8,128)}, u32[]{:S(2)}) copy-start(f32[1,4,16,512]{3,2,1,0:T(8,128)} %param.12) | copy-start | bytes 393220
  128.6 14.1 %copy-start.6 = (f32[1,4,16,512]{3,2,1,0:T(8,128)S(1)}, f32[1,4,16,512]{3,2,1,0:T(8,128)}, u32[]{:S(2)}) copy-start(f32[1,4,16,512]{3,2,1,0:T(8,128)} %param.13) | copy-start | bytes 393220
  128.6 14.1 %copy-start.8 = (s32[1,1,2]{2,1,0:T(1,128)S(1)}, s32[1,1,2]{2,1,0:T(1,128)}, u32[]{:S(2)}) copy-start(s32[1,1,2]{2,1,0:T(1,128)} %param.14) | copy-start | bytes 28
  128.6 15.5 %collective-permute-start.5 = (bf16[256,512]{1,0:T(8,128)(2,1)}, bf16[256,512]{1,0:T(8,128)(2,1)}, u32[]{:S(2)}, u32[]{:S(2)}) collective-permute-start(bf16[256,512]{1,0:T(8,128)(2,1)} %fusion.7), channel_id=1, source_target_pairs={{128,0},{0,128},{384,256},{129,1},{1,129},{385,257},{130,2},{2,130... | collective-permute-start | bytes 786440 | tf_op jit(solution)/shard_map/ppermute | solution.py:387
  132.2 10.5 %all-to-all-start.4 = ((bf16[4,5,16,512]{3,2,1,0:T(8,128)(2,1)}), bf16[4,5,16,512]{3,2,1,0:T(8,128)(2,1)S(1)}, u32[]{:S(2)}, u32[]{:S(2)}) async-start(bf16[4,5,16,512]{3,2,1,0:T(8,128)(2,1)} %shard_map.125), calls=%async_computation.4 | async-start | bytes 655360 | tf_op jit(solution)/shard_map/all_to_all | solution.py:21
  135.7 9.4 %copy-start.4 = (f32[256,512]{1,0:T(8,128)S(1)}, f32[256,512]{1,0:T(8,128)}, u32[]{:S(2)}) copy-start(f32[256,512]{1,0:T(8,128)} %copy-done.3) | copy-start | bytes 1572868
  138.2 8.1 %copy-start.18 = (bf16[256,512]{1,0:T(8,128)(2,1)S(1)}, bf16[256,512]{1,0:T(8,128)(2,1)}, u32[]{:S(2)}) copy-start(bf16[256,512]{1,0:T(8,128)(2,1)} %get-tuple-element.71) | copy-start | bytes 786436
  138.2 8.1 %copy-start.19 = (bf16[256,512]{1,0:T(8,128)(2,1)S(1)}, bf16[256,512]{1,0:T(8,128)(2,1)}, u32[]{:S(2)}) copy-start(bf16[256,512]{1,0:T(8,128)(2,1)} %get-tuple-element.72) | copy-start | bytes 786436
Sparse Core Ops, SparseCore 0:
  22.3 46.9 all-gather.6
  72.4 49.1 all-gather.8
